TPU v7x, 512 devices: a whole 4x8x8 slice. The times are simulated.
512 devices in a mesh: var: 32 (over y_lo, z), lon: 16 (over x, y_hi, core).
Axes of the slice: x: 4, y: 8 (y_hi: 2, y_lo: 4; y = y_hi * 4 + y_lo), z: 8, core: 2. Of those that a mesh axis runs over, the one named last changes fastest.
Arguments:
- pixels: bfloat16 [32, 768, 768], P('var', None, 'lon'), may hold values from -50 to 50
- embed_weight: bfloat16 [4, 16, 512], replicated, may hold values from -0.75 to 0.75
- level_code: float32 [8, 512], replicated, may hold values from -6 to 6
- queries: bfloat16 [3, 512], replicated, may hold values from -6 to 6
- w_key: bfloat16 [512, 512], replicated, may hold values from -0.25 to 0.25
- w_value: bfloat16 [512, 512], replicated, may hold values from -0.25 to 0.25
- w_out: bfloat16 [512, 512], replicated, may hold values from -0.25 to 0.25
- w_qkv: bfloat16 [512, 1536], replicated, may hold values from -0.25 to 0.25
- w_proj: bfloat16 [512, 512], replicated, may hold values from -0.25 to 0.25
Outputs:
- encoded: bfloat16 [3, 192, 192, 512], P(None, 'var', 'lon')
All inputs are finite; a program needn't handle non-finite values.
Results may differ from a plain program's by a relative error of at most 0.017.
Values may be sent and summed in bfloat16 or wider, within the bound.
No kernel may reach another device: no remote copies, remote signals or barrier semaphores. Data moves between devices by JAX's collectives and lax.ppermute only.
A program may use at most 64 MiB of HBM per device.

v0:
```python
import jax
import jax.numpy as jnp
from jax import lax
from jax.sharding import PartitionSpec as P

HEAD = 64
LATENT = 3
WLAT = 6
WLON = 12


def from_behind(value, axis, by):
    devices = lax.axis_size(axis)
    return lax.ppermute(value, axis, [(i, (i + by) % devices) for i in range(devices)])


def norm_rows(values_in):
    center = values_in - jnp.mean(values_in, axis=-1, keepdims=True)
    spread = jnp.mean(center * center, axis=-1, keepdims=True)
    return center * lax.rsqrt(spread + 1e-05)


def to_patches(pixel_block):
    count, rows, cols = pixel_block.shape
    shaped = pixel_block.reshape(count, rows // 4, 4, cols // 4, 4)
    return shaped.transpose(0, 1, 3, 2, 4).reshape(count, rows // 4, cols // 4, 16)


def embed(patch_block, field_weights):
    product = jnp.einsum(
        "fabk,fkd->fabd", patch_block, field_weights, preferred_element_type=jnp.float32
    )
    return product.astype(jnp.bfloat16)


def aggregate(embedded, level_code, queries, w_key, w_value, w_out):
    count, rows, cols, width = embedded.shape
    levels = level_code.shape[0]
    heads = width // HEAD
    token = (
        embedded.astype(jnp.float32).reshape(levels, count // levels, rows, cols, width).sum(axis=1)
    )
    token = token + level_code[:, None, None, :]
    normed = norm_rows(token).astype(jnp.bfloat16).reshape(-1, width)
    keys = jnp.dot(normed, w_key, preferred_element_type=jnp.float32).astype(jnp.bfloat16)
    values = jnp.dot(normed, w_value, preferred_element_type=jnp.float32).astype(jnp.bfloat16)
    keys = keys.reshape(levels, rows, cols, heads, HEAD)
    values = values.reshape(levels, rows, cols, heads, HEAD)
    query_heads = queries.reshape(LATENT, heads, HEAD)
    scores = jnp.einsum(
        "qhe,labhe->abhql", query_heads, keys, preferred_element_type=jnp.float32
    ) * HEAD ** (-0.5)
    expo = jnp.exp(scores)
    level_weights = (expo / jnp.sum(expo, axis=-1, keepdims=True)).astype(jnp.bfloat16)
    attended = jnp.einsum(
        "abhql,labhe->qabhe", level_weights, values, preferred_element_type=jnp.float32
    )
    attended = attended.astype(jnp.bfloat16).reshape(-1, width)
    projected = jnp.dot(attended, w_out, preferred_element_type=jnp.float32).reshape(
        LATENT, rows, cols, width
    )
    return (queries.astype(jnp.float32)[:, None, None, :] + projected).astype(jnp.bfloat16)


def window_layer(latent, w_qkv, w_proj):
    levels, rows, cols, width = latent.shape
    heads = width // HEAD
    row_blocks = rows // WLAT
    col_blocks = cols // WLON
    windows = latent.reshape(levels, row_blocks, WLAT, col_blocks, WLON, width).transpose(
        1, 3, 0, 2, 4, 5
    )
    windows = windows.reshape(row_blocks * col_blocks, levels * WLAT * WLON, width)
    count, members, _ = windows.shape
    normed = norm_rows(windows.astype(jnp.float32)).astype(jnp.bfloat16).reshape(-1, width)
    qkv = jnp.dot(normed, w_qkv, preferred_element_type=jnp.float32).astype(jnp.bfloat16)
    qkv = qkv.reshape(count, members, 3, heads, HEAD)
    scores = jnp.einsum(
        "wnhe,wmhe->whnm", qkv[:, :, 0], qkv[:, :, 1], preferred_element_type=jnp.float32
    ) * HEAD ** (-0.5)
    expo = jnp.exp(scores)
    probs = (expo / jnp.sum(expo, axis=-1, keepdims=True)).astype(jnp.bfloat16)
    mixed = jnp.einsum(
        "whnm,wmhe->wnhe", probs, qkv[:, :, 2], preferred_element_type=jnp.float32
    ).astype(jnp.bfloat16)
    projected = jnp.dot(mixed.reshape(-1, width), w_proj, preferred_element_type=jnp.float32)
    summed = (windows.astype(jnp.float32).reshape(-1, width) + projected).astype(jnp.bfloat16)
    summed = summed.reshape(row_blocks, col_blocks, levels, WLAT, WLON, width).transpose(
        2, 0, 3, 1, 4, 5
    )
    return summed.reshape(levels, rows, cols, width)


def body(pixels, embed_weight, level_code, queries, w_key, w_value, w_out, w_qkv, w_proj):
    half_window = WLON // 2
    patch_block = to_patches(pixels)
    fields_here = patch_block.shape[0]
    variables = embed_weight.shape[0]
    field_ids = lax.axis_index("var") * fields_here + jnp.arange(fields_here, dtype=jnp.int32)
    selector = (
        field_ids[:, None] % variables == jnp.arange(variables, dtype=jnp.int32)[None, :]
    ).astype(jnp.float32)
    chosen = jnp.einsum("fv,vkd->fkd", selector, embed_weight.astype(jnp.float32)).astype(
        jnp.bfloat16
    )
    embedded = embed(patch_block, chosen)
    aggregate_embedded = lax.all_to_all(embedded, "var", split_axis=1, concat_axis=0, tiled=True)
    latent = aggregate(aggregate_embedded, level_code, queries, w_key, w_value, w_out)
    edge_latent = from_behind(latent[:, :, :half_window], "lon", -1)
    latent = jnp.concatenate([latent[:, :, half_window:], edge_latent], axis=2)
    return window_layer(latent, w_qkv, w_proj)


def solution(mesh):
    placed = (P("var", None, "lon"), P(), P(), P(), P(), P(), P(), P(), P())
    return jax.shard_map(
        body, mesh=mesh, in_specs=placed, out_specs=P(None, "var", "lon", None), check_vma=False
    )
```

profile of v0, /device:TPU:75, one launch (start us, length us, event | category | flops | bytes accessed | tf_op | source)
XLA Modules:
  0.0 188.7 jit_solution(18144919315113874728)
XLA Ops:
  0.0 6.9 %reshape.195 = bf16[1,192,4,12,4]{2,1,4,3,0:T(8,128)(2,1)} reshape(bf16[1,768,48]{1,2,0:T(8,128)(2,1)} %param.9) | data formatting | bytes 147456 | tf_op jit(solution)/shard_map/reshape | solution.py:25
  6.9 2.4 %copy.59 = bf16[1,192,12,4,4]{1,4,3,2,0:T(4,128)(2,1)S(1)} copy(bf16[1,192,12,4,4]{3,1,4,2,0:T(8,128)(2,1)} %bitcast.65) | data formatting | bytes 147456 | tf_op jit(solution)/shard_map/transpose | solution.py:26
  9.6 0.8 convert_bitcast_fusion
  10.4 3.1 %copy.60 = bf16[1,192,12,512]{3,2,0,1:T(8,128)(2,1)} copy(bf16[1,192,12,512]{3,1,2,0:T(8,128)(2,1)S(1)} %convert_bitcast_fusion) | data formatting | bytes 4718592 | tf_op jit(solution)/shard_map/convert_element_type | solution.py:33
  13.5 12.7 %all-to-all-start = ((bf16[1,192,12,512]{3,2,0,1:T(8,128)(2,1)}), bf16[1,192,12,512]{3,2,0,1:T(8,128)(2,1)}, u32[]{:S(2)}, u32[]{:S(2)}) async-start(bf16[1,192,12,512]{3,2,0,1:T(8,128)(2,1)} %copy.60), calls=%async_computation | async-start | bytes 6291456 | tf_op jit(solution)/shard_map/all_to_all | solution.py:107
  26.3 80.7 %all-to-all-done = bf16[1,192,12,512]{3,2,0,1:T(8,128)(2,1)} async-done(((bf16[1,192,12,512]{3,2,0,1:T(8,128)(2,1)}), bf16[1,192,12,512]{3,2,0,1:T(8,128)(2,1)}, u32[]{:S(2)}, u32[]{:S(2)}) %all-to-all-start) | async-done | bytes 2359328 | tf_op jit(solution)/shard_map/all_to_all | solution.py:107
  107.0 5.5 %copy_convert_fusion = f32[1,192,12,512]{3,1,2,0:T(8,128)} fusion(bf16[1,192,12,512]{3,2,0,1:T(8,128)(2,1)} %all-to-all-done), kind=kLoop, calls=%fused_computation.1 | loop fusion | flops 1179648 | bytes 7077888 | tf_op jit(solution)/shard_map/convert_element_type | solution.py:41
  112.5 6.5 %reshape.205 = f32[8,4,6,12,512]{4,2,1,0,3:T(8,128)} reshape(f32[1,192,12,512]{3,1,2,0:T(8,128)} %copy_convert_fusion) | data formatting | bytes 9437184 | tf_op jit(solution)/shard_map/convert_element_type | solution.py:41
  119.0 4.9 %reduce_sum.63 = f32[8,6,12,512]{3,1,0,2:T(8,128)} reduce(f32[8,4,6,12,512]{4,2,1,0,3:T(8,128)} %reshape.205, f32[]{:T(128)} %constant.36.clone.1), dimensions={1}, to_apply=%region_0.1 | reduce | flops 884736 | bytes 5898244 | tf_op jit(solution)/shard_map/reduce_sum | solution.py:41
  124.0 1.7 fusion.29
  125.9 1.9 copy.62
  128.4 1.5 add.56
  130.0 1.6 convolution_convert_fusion.3
  131.6 1.6 reshape.197
  133.2 1.6 convolution_convert_fusion.2
  135.4 3.8 %fusion.31 = (f32[6,12,8,3]{1,3,0,2:T(4,128)S(1)}, f32[6,12,8,3,8]{1,3,0,4,2:T(4,128)S(1)}) fusion(bf16[3,8,64,1,1]{2,1,0,4,3:T(8,128)(2,1)S(1)} %bitcast.69, bf16[8,6,12,8,64]{4,3,2,1,0:T(8,128)(2,1)S(1)} %reshape.198), kind=kOutput, calls=%fused_computation.51 | convolution fusion | flops 1795392 | bytes 655104 | tf_op jit(solution)/shard_map/qhe,labhe->abhql/dot_general | solution.py:50
  139.3 2.5 %copy.71 = bf16[6,12,8,3,8]{4,3,2,1,0:T(4,128)(2,1)} copy(bf16[6,12,8,3,8]{1,3,0,4,2:T(4,128)(2,1)S(1)} %divide_convert_fusion.2) | data formatting | bytes 55296 | tf_op jit(solution)/shard_map/convert_element_type | solution.py:54
  141.8 2.1 %fusion.12 = bf16[3,6,12,8,64]{4,0,3,2,1:T(4,128)(2,1)S(1)} fusion(bf16[6,12,8,3,8]{4,3,2,1,0:T(4,128)(2,1)} %copy.71, bf16[8,6,12,8,64]{4,3,2,1,0:T(8,128)(2,1)S(1)} %copy-done.1), kind=kOutput, calls=%fused_computation.15 | convolution fusion | flops 1880064 | bytes 838656 | tf_op jit(solution)/shard_map/abhql,labhe->qabhe/dot_general | solution.py:55
  145.3 4.5 %collective-permute-start = (bf16[3,6,6,512]{3,2,1,0:T(8,128)(2,1)S(1)}, bf16[3,6,6,512]{3,2,1,0:T(8,128)(2,1)S(1)}, u32[]{:S(2)}, u32[]{:S(2)}) collective-permute-start(bf16[3,6,6,512]{3,2,1,0:T(8,128)(2,1)S(1)} %get-tuple-element.8), channel_id=1, source_target_pairs={{0,15},{1,0},{2,1},{3,2},{4,3},{5,4},{6,5},{7,6},{8,7},{9,8},{10,9... | collective-permute-start | bytes 331784 | tf_op jit(solution)/shard_map/ppermute | solution.py:14
  149.9 32.3 %collective-permute-done = bf16[3,6,6,512]{3,2,1,0:T(8,128)(2,1)S(1)} collective-permute-done((bf16[3,6,6,512]{3,2,1,0:T(8,128)(2,1)S(1)}, bf16[3,6,6,512]{3,2,1,0:T(8,128)(2,1)S(1)}, u32[]{:S(2)}, u32[]{:S(2)}) %collective-permute-start) | collective-permute-done | bytes 110624 | tf_op jit(solution)/shard_map/ppermute | solution.py:14
  183.5 1.2 copy.73
  184.6 1.5 fusion.2
  186.2 1.5 convolution_convert_fusion.4
  188.0 0.8 reshape_transpose_reshape.4
  (44 shorter events, 5.0 us)
Async XLA Ops:
  0.0 182.9 %copy-start = (bf16[512,1536]{1,0:T(8,128)(2,1)S(1)}, bf16[512,1536]{1,0:T(8,128)(2,1)}, u32[]{:S(2)}) copy-start(bf16[512,1536]{1,0:T(8,128)(2,1)} %param.16) | copy-start | bytes 4718596
  6.9 2.5 %copy-start.6 = (bf16[4,16,512]{2,1,0:T(8,128)(2,1)S(1)}, bf16[4,16,512]{2,1,0:T(8,128)(2,1)}, u32[]{:S(2)}) copy-start(bf16[4,16,512]{2,1,0:T(8,128)(2,1)} %param.10) | copy-start | bytes 196612
  13.5 12.7 %copy-start.5 = (bf16[3,512]{1,0:T(4,128)(2,1)S(1)}, bf16[3,512]{1,0:T(4,128)(2,1)}, u32[]{:S(2)}) copy-start(bf16[3,512]{1,0:T(4,128)(2,1)} %param.12) | copy-start | bytes 9220
  13.5 93.5 %all-to-all-start = ((bf16[1,192,12,512]{3,2,0,1:T(8,128)(2,1)}), bf16[1,192,12,512]{3,2,0,1:T(8,128)(2,1)}, u32[]{:S(2)}, u32[]{:S(2)}) async-start(bf16[1,192,12,512]{3,2,0,1:T(8,128)(2,1)} %copy.60), calls=%async_computation | async-start | bytes 6291456 | tf_op jit(solution)/shard_map/all_to_all | solution.py:107
  119.0 4.9 %copy-start.4 = (f32[8,512]{1,0:T(8,128)S(1)}, f32[8,512]{1,0:T(8,128)}, u32[]{:S(2)}) copy-start(f32[8,512]{1,0:T(8,128)} %param.11) | copy-start | bytes 49156
  139.2 2.7 %copy-start.1 = (bf16[8,6,12,8,64]{4,3,2,1,0:T(8,128)(2,1)S(1)}, bf16[8,6,12,8,64]{4,3,2,1,0:T(8,128)(2,1)}, u32[]{:S(2)}) copy-start(bf16[8,6,12,8,64]{4,3,2,1,0:T(8,128)(2,1)} %reshape.197) | copy-start | bytes 1769476
  143.9 1.0 copy-start.2
  145.3 36.8 %collective-permute-start = (bf16[3,6,6,512]{3,2,1,0:T(8,128)(2,1)S(1)}, bf16[3,6,6,512]{3,2,1,0:T(8,128)(2,1)S(1)}, u32[]{:S(2)}, u32[]{:S(2)}) collective-permute-start(bf16[3,6,6,512]{3,2,1,0:T(8,128)(2,1)S(1)} %get-tuple-element.8), channel_id=1, source_target_pairs={{0,15},{1,0},{2,1},{3,2},{4,3},{5,4},{6,5},{7,6},{8,7},{9,8},{10,9... | collective-permute-start | bytes 331784 | tf_op jit(solution)/shard_map/ppermute | solution.py:14
  186.2 1.5 copy-start.3
where the time goes:
time: 189 us
  waiting for transfers between devices  113 us (60%)
  local copies, waits for them, and re-layouts  31 us (16%)
  starting transfers between devices  17.2 us (9%)
  matrix products  14.2 us (8%)
  other arithmetic  13.1 us (7%)
    all_to_all x1, waiting for transfers between devices, body(): lax.all_to_all(embedded, 'var', split_axis=1, concat_axis=0, tiled=True)  80.7 us
    ppermute x1, waiting for transfers between devices, from_behind(): lax.ppermute(value, axis, [(i, (i + by) % devices) for i in range(devices)])  32.3 us
    all_to_all x1, starting transfers between devices, body(): lax.all_to_all(embedded, 'var', split_axis=1, concat_axis=0, tiled=True)  12.7 us
    reshape x1, local copies, waits for them, and re-layouts, to_patches(): shaped = pixel_block.reshape(count, rows // 4, 4, cols // 4, 4)  6.87 us
    convert_element_type x1, local copies, waits for them, and re-layouts, aggregate(): embedded.astype(jnp.float32)  6.54 us
    convert_element_type x1, other arithmetic, aggregate(): embedded.astype(jnp.float32)  5.48 us
    reduce_sum x1, other arithmetic, aggregate(): embedded.astype(jnp.float32)  4.94 us
    ppermute x1, starting transfers between devices, from_behind(): lax.ppermute(value, axis, [(i, (i + by) % devices) for i in range(devices)])  4.52 us
  transfers between devices with their start and end apart: 2, of which 2 were waited for; matrix products, arithmetic and copies ran while one was open for 0% of the time, Pallas kernels for 0%

commit v1 on v0

v1 whole, which is shorter than its diff:
```python
import jax
import jax.numpy as jnp
from jax import lax
from jax.experimental import pallas as pl
from jax.experimental.pallas import tpu as pltpu
from jax.sharding import PartitionSpec as P

HEAD = 64
LATENT = 3
WLAT = 6
WLON = 12
HALF = WLON // 2
PATCH = 4
SLOT = 8
LANES = 128
GROUP = 32
LOG2E = 1.4426950408889634
F32 = jnp.float32
BF16 = jnp.bfloat16


def mul(a, b):
    return jnp.dot(a, b, preferred_element_type=F32)


def mul_t(a, b):
    return lax.dot_general(a, b, (((1,), (1,)), ((), ())), preferred_element_type=F32)


def iota(shape, dim):
    return lax.broadcasted_iota(jnp.int32, shape, dim)


def split(value):
    high = value.astype(BF16).astype(F32)
    return high, value - high


def pack_kernel(pixel_ref, out_ref, rows):
    count, cols = pixel_ref.shape
    band = PATCH * WLAT
    bands = count // band
    rows[pl.ds(0, count), pl.ds(0, cols)] = pixel_ref[...].astype(F32)
    rows[pl.ds(count, 16), :] = jnp.zeros((16, LANES), F32)
    source, target = iota((cols, 2 * LANES), 0), iota((cols, 2 * LANES), 1)
    base = source // (cols // 2) * LANES + source % (cols // 2)
    total = None
    for r in range(PATCH):
        picked = jnp.concatenate(
            [rows[pl.ds(band * g + r, SLOT, stride=PATCH), :] for g in range(bands)], axis=0
        )[:, :cols].astype(BF16)
        place = jnp.where(target == base + r * GROUP, 1.0, 0.0).astype(BF16)
        part = mul(picked, place)
        total = part if total is None else total + part
    west = total[:, :LANES].reshape(bands, SLOT, LANES)
    own = total[:, LANES:].reshape(bands, SLOT, LANES)
    out_ref[...] = (
        jnp.concatenate([west, own], axis=1).reshape(bands * 2 * SLOT, LANES).astype(BF16)
    )


def fold_weights(embed_ref, level_ref, query_ref, key_ref, value_ref):
    pixels, width = embed_ref.shape
    levels = level_ref.shape[0]
    ext = jnp.concatenate([embed_ref[...].astype(F32), level_ref[...]], axis=0)
    count = pixels + levels
    ext = ext - jnp.mean(ext, axis=-1, keepdims=True)
    high, low = split(ext)
    stacked = jnp.concatenate([high, low], axis=0).astype(BF16)
    keys = mul(stacked, key_ref[...])
    keys = keys[:count] + keys[count:]
    values = mul(stacked, value_ref[...])
    values = values[:count] + values[count:]
    heads = width // HEAD
    scores = None
    for q in range(LATENT):
        high_q, low_q = split(keys * query_ref[pl.ds(q, 1), :].astype(F32))
        both = jnp.concatenate([high_q, low_q], axis=0).astype(BF16)
        collect = jnp.where(
            iota((width, LANES), 1) == q * heads + iota((width, LANES), 0) // HEAD, 1.0, 0.0
        ).astype(BF16)
        part = mul(both, collect)
        part = part[:count] + part[count:]
        scores = part if scores is None else scores + part
    scores = scores * (HEAD ** (-0.5) * LOG2E)
    zeros = jnp.zeros((LANES - count, width), F32)
    high_t = jnp.concatenate([high, zeros], axis=0).astype(BF16)
    low_t = jnp.concatenate([low, zeros], axis=0).astype(BF16)
    high_b, low_b = high.astype(BF16), low.astype(BF16)
    gram = (mul_t(high_b, high_t) + (mul_t(high_b, low_t) + mul_t(low_b, high_t))) * (1.0 / width)
    row, lane = iota((count, LANES), 0), iota((count, LANES), 1)
    diagonal = jnp.sum(jnp.where(row == lane, gram, 0.0), axis=-1, keepdims=True)
    spread = jnp.where(row < pixels, gram, 2.0 * gram)
    spread = jnp.where(
        lane < pixels, spread, jnp.where((lane == pixels) & (row >= pixels), diagonal, 0.0)
    )
    folded = jnp.concatenate([values, spread, scores], axis=1)
    high_f, low_f = split(folded)
    rest = jnp.zeros((2 * LANES - 2 * count, folded.shape[1]), F32)
    return jnp.concatenate(
        [high_f[:pixels], low_f[:pixels], high_f[pixels:], low_f[pixels:], rest], axis=0
    ).astype(BF16)


def aggregate_half(rows, folded, query_ref, out_weight, levels):
    variables = rows.shape[0] // levels
    width = out_weight.shape[0]
    heads = width // HEAD
    pixels = variables * PATCH * PATCH
    grid = rows.reshape(levels, variables, SLOT, LANES)
    wide = jnp.concatenate(
        [grid[:, v].reshape(levels * SLOT, LANES) for v in range(variables)], axis=1
    )
    depth = variables * LANES
    column = iota((1, depth), 1) % GROUP // PATCH
    masked = jnp.concatenate(
        [jnp.where(column == b, wide, 0.0) for b in range(HALF)], axis=0
    ).astype(BF16)
    source, target = iota((depth, LANES), 0), iota((depth, LANES), 1)
    place = (
        source // LANES * (PATCH * PATCH) + source % LANES // GROUP * PATCH + source % PATCH
    )
    gather = jnp.where(target % pixels == place, 1.0, 0.0).astype(BF16)
    patch = mul(masked, gather)
    count = HALF * levels * SLOT
    row, lane = iota((count, LANES), 0), iota((count, LANES), 1)
    level = jnp.where(
        (lane < 2 * levels) & (lane % levels == row // SLOT % levels), 1.0, 0.0
    )
    full = jnp.concatenate([patch, level], axis=1).astype(BF16)
    product = mul(full, folded)
    values = product[:, :width]
    spread = product[:, width : width + LANES]
    scores = product[:, width + LANES :]
    variance = jnp.sum(jnp.where(lane == pixels, 1.0, patch) * spread, axis=-1, keepdims=True)
    scale = lax.rsqrt(jnp.maximum(variance, 0.0) + 1e-05)
    expo = jnp.exp2(scores * scale).reshape(HALF, levels, SLOT, LANES)
    weights = expo / jnp.sum(expo, axis=1, keepdims=True) * scale.reshape(HALF, levels, SLOT, 1)
    weights = weights.reshape(count, LANES).astype(BF16)
    mixed = []
    for q in range(LATENT):
        spread_out = jnp.where(
            iota((LANES, width), 0) == q * heads + iota((LANES, width), 1) // HEAD, 1.0, 0.0
        ).astype(BF16)
        part = mul(weights, spread_out) * values
        mixed.append(part.reshape(HALF, levels, SLOT, width).sum(axis=1).reshape(HALF * SLOT, width))
    attended = jnp.concatenate(mixed, axis=0).astype(BF16)
    latent = mul(attended, out_weight).reshape(LATENT, HALF * SLOT, width)
    latent = latent + query_ref[...].astype(F32)[:, None, :]
    return latent.astype(BF16).astype(F32)


def own_kernel(
    block_ref, embed_ref, level_ref, query_ref, key_ref, value_ref, out_w_ref, latent_ref, folded_ref
):
    folded = fold_weights(embed_ref, level_ref, query_ref, key_ref, value_ref)
    folded_ref[...] = folded
    fields = block_ref.shape[0] // (2 * SLOT)
    rows = block_ref[...].astype(F32).reshape(fields, 2, SLOT, LANES)[:, 1]
    latent_ref[...] = aggregate_half(rows, folded, query_ref, out_w_ref[...], level_ref.shape[0])


def window_kernel(
    block_ref, own_ref, folded_ref, query_ref, out_w_ref, qkv_w_ref, proj_w_ref, out_ref, slots, clean
):
    fields = block_ref.shape[0] // SLOT
    width = out_w_ref.shape[0]
    levels = fields // 4
    rows = block_ref[...].astype(F32).reshape(fields, SLOT, LANES)
    east = aggregate_half(rows, folded_ref[...], query_ref, out_w_ref[...], levels)
    half_rows = HALF * SLOT
    for q in range(LATENT):
        for c in range(width // LANES):
            part = pl.ds(c * LANES, LANES)
            slots[c, pl.ds(q * 2 * half_rows, half_rows), :] = own_ref[q, :, part]
            slots[c, pl.ds(q * 2 * half_rows + half_rows, half_rows), :] = east[
                q, :, c * LANES : (c + 1) * LANES
            ]
    for q in range(LATENT):
        for a in range(WLAT):
            for c in range(width // LANES):
                clean[pl.ds((q * WLAT + a) * WLON, WLON), pl.ds(c * LANES, LANES)] = slots[
                    c, pl.ds(q * 2 * half_rows + a, WLON, stride=SLOT), :
                ]
    members = LATENT * WLAT * WLON
    shifted = clean[...]
    center = shifted - jnp.mean(shifted, axis=-1, keepdims=True)
    spread = jnp.mean(center * center, axis=-1, keepdims=True)
    normed = (center * lax.rsqrt(spread + 1e-05)).astype(BF16)
    qkv = mul(normed, qkv_w_ref[...]).astype(BF16)
    first = iota((1, LANES), 1) < HEAD
    mixed = []
    for p in range(width // LANES):
        queries = qkv[:, p * LANES : (p + 1) * LANES]
        keys = qkv[:, width + p * LANES : width + (p + 1) * LANES]
        values = qkv[:, 2 * width + p * LANES : 2 * width + (p + 1) * LANES]
        values = jnp.concatenate(
            [values * BF16(2.0**-8), jnp.ones((members, LANES), BF16)], axis=1
        )
        found = []
        for keep in (first, jnp.logical_not(first)):
            chosen = jnp.where(keep, queries, jnp.zeros_like(queries))
            scores = mul_t(chosen, keys)
            expo = jnp.exp2(scores * (HEAD ** (-0.5) * LOG2E)).astype(BF16)
            found.append(mul(expo, values))
        both = jnp.where(jnp.concatenate([first, first], axis=1), found[0], found[1])
        mixed.append((both[:, :LANES] / both[:, LANES:] * 2.0**8).astype(BF16))
    projected = mul(jnp.concatenate(mixed, axis=1), proj_w_ref[...])
    clean[...] = shifted + projected
    for q in range(LATENT):
        for a in range(WLAT):
            out_ref[q, a] = clean[pl.ds((q * WLAT + a) * WLON, WLON), :].astype(BF16)


def whole(count):
    return [pl.BlockSpec(memory_space=pltpu.VMEM)] * count


def body(pixels, embed_weight, level_code, queries, w_key, w_value, w_out, w_qkv, w_proj):
    _, count, cols = pixels.shape
    bands = count // (PATCH * WLAT)
    width = w_out.shape[0]
    packed = pl.pallas_call(
        pack_kernel,
        out_shape=jax.ShapeDtypeStruct((bands * 2 * SLOT, LANES), BF16),
        in_specs=whole(1),
        out_specs=whole(1)[0],
        scratch_shapes=[pltpu.VMEM((count + 16, LANES), F32)],
        name="pack",
    )(pixels[0])
    block = lax.all_to_all(
        packed.reshape(bands, 2 * SLOT, LANES), "var", split_axis=0, concat_axis=0, tiled=True
    )
    sectors = lax.axis_size("lon")
    east = lax.ppermute(block[:, :SLOT], "lon", [(i, (i - 1) % sectors) for i in range(sectors)])
    fields = block.shape[0]
    own, folded = pl.pallas_call(
        own_kernel,
        out_shape=[
            jax.ShapeDtypeStruct((LATENT, HALF * SLOT, width), F32),
            jax.ShapeDtypeStruct((2 * LANES, width + 2 * LANES), BF16),
        ],
        in_specs=whole(7),
        out_specs=whole(2),
        compiler_params=pltpu.CompilerParams(vmem_limit_bytes=24 * 2**20),
        cost_estimate=pl.CostEstimate(flops=4 * 10**9, bytes_accessed=2 * 10**6, transcendentals=0),
        name="own_half",
    )(
        block.reshape(fields * 2 * SLOT, LANES),
        embed_weight.reshape(-1, width),
        level_code,
        queries,
        w_key,
        w_value,
        w_out,
    )
    return pl.pallas_call(
        window_kernel,
        out_shape=jax.ShapeDtypeStruct((LATENT, WLAT, WLON, width), BF16),
        in_specs=whole(7),
        out_specs=whole(1)[0],
        scratch_shapes=[
            pltpu.VMEM((width // LANES, LATENT * WLON * SLOT, LANES), F32),
            pltpu.VMEM((LATENT * WLAT * WLON, width), F32),
        ],
        compiler_params=pltpu.CompilerParams(vmem_limit_bytes=32 * 2**20),
        cost_estimate=pl.CostEstimate(flops=8 * 10**9, bytes_accessed=4 * 10**6, transcendentals=0),
        name="window",
    )(east.reshape(fields * SLOT, LANES), own, folded, queries, w_out, w_qkv, w_proj)


def solution(mesh):
    placed = (P("var", None, "lon"), P(), P(), P(), P(), P(), P(), P(), P())
    return jax.shard_map(
        body, mesh=mesh, in_specs=placed, out_specs=P(None, "var", "lon", None), check_vma=False
    )
```

time: 189 us -> 43.3 us (0.23)
  the two profiles are of different devices: /device:TPU:75 before, /device:TPU:8 now
where the time goes in v1:
time: 43.3 us; the launch traced here: 42.8 us
  blocking collectives  23.3 us (54%)
  local copies, waits for them, and re-layouts  7.08 us (16%)
  Pallas kernels  7.06 us (16%)
  starting transfers between devices  5.29 us (12%)
    all_to_all x1, blocking collectives, body(): lax.all_to_all(packed.reshape(bands, 2 * SLOT, LANES), 'var', split_axis=...  23.3 us
    unnamed x21, local copies, waits for them, and re-layouts  7.07 us
    ppermute x1, starting transfers between devices, body(): lax.ppermute(block[:, :SLOT], 'lon', [(i, (i - 1) % sectors) for i in ran...  5.29 us
    pallas_call x1, Pallas kernels, body(): pl.pallas_call(window_kernel, out_shape=jax.ShapeDtypeStruct((LATENT, WLA...  3.41 us
    pallas_call x1, Pallas kernels, body(): pl.pallas_call(pack_kernel, out_shape=jax.ShapeDtypeStruct((bands * 2 * S...  1.86 us
    pallas_call x1, Pallas kernels, body(): pl.pallas_call(own_kernel, out_shape=[jax.ShapeDtypeStruct((LATENT, HALF...  1.79 us
  transfers between devices with their start and end apart: 1, of which 0 were waited for; matrix products, arithmetic and copies ran while one was open for 0% of the time, Pallas kernels for 4%

profile of v1, /device:TPU:8, one launch (start us, length us, event | category | flops | bytes accessed | tf_op | source)
XLA Modules:
  0.0 42.8 jit_solution(398340163175038251)
XLA Ops:
  0.0 1.7 %copy.10 = bf16[1,768,48]{2,1,0:T(8,128)(2,1)} copy(bf16[1,768,48]{1,2,0:T(8,128)(2,1)} %param.9) | data formatting | bytes 147456 | tf_op args[0]
  1.7 1.9 %pack.1 = bf16[512,128]{1,0:T(8,128)(2,1)} custom-call(bf16[768,48]{1,0:T(8,128)(2,1)} %bitcast.8), custom_call_target="tpu_custom_call" | custom-call | tf_op jit(solution)/shard_map/pack/pallas_call | solution.py:223
  3.6 23.3 %all_to_all.5 = bf16[32,16,128]{2,1,0:T(8,128)(2,1)S(1)} all-to-all(bf16[32,16,128]{2,1,0:T(8,128)(2,1)} %bitcast.9), channel_id=1, replica_groups=mesh['var'=32,'lon'=16] {'var'}, dimensions={0} | all-to-all | bytes 262144 | tf_op jit(solution)/shard_map/all_to_all | solution.py:231
  26.9 5.3 %collective-permute-start = (bf16[32,8,128]{2,1,0:T(8,128)(2,1)S(1)}, bf16[32,8,128]{2,1,0:T(8,128)(2,1)S(1)}, u32[]{:S(2)}, u32[]{:S(2)}) collective-permute-start(bf16[32,8,128]{2,1,0:T(8,128)(2,1)S(1)} %slice.4), channel_id=1, source_target_pairs={{0,15},{1,0},{2,1},{3,2},{4,3},{5,4},{6,5},{7,6},{8,7},{9,8},{10,9... | collective-permute-start | bytes 196616 | tf_op jit(solution)/shard_map/ppermute | solution.py:235
  32.2 0.0 copy-start.1
  32.2 1.0 %copy-done.1 = bf16[512,512]{1,0:T(8,128)(2,1)S(1)} copy-done((bf16[512,512]{1,0:T(8,128)(2,1)S(1)}, bf16[512,512]{1,0:T(8,128)(2,1)}, u32[]{:S(2)}) %copy-start.1) | copy-done | bytes 524312
  33.2 0.0 copy-start.2
  33.2 1.0 %copy-done.2 = bf16[512,512]{1,0:T(8,128)(2,1)S(1)} copy-done((bf16[512,512]{1,0:T(8,128)(2,1)S(1)}, bf16[512,512]{1,0:T(8,128)(2,1)}, u32[]{:S(2)}) %copy-start.2) | copy-done | bytes 524312
  34.3 0.0 copy-start.3
  34.3 1.0 %copy-done.3 = bf16[512,512]{1,0:T(8,128)(2,1)S(1)} copy-done((bf16[512,512]{1,0:T(8,128)(2,1)S(1)}, bf16[512,512]{1,0:T(8,128)(2,1)}, u32[]{:S(2)}) %copy-start.3) | copy-done | bytes 524312
  35.3 0.8 %copy-done.6 = bf16[4,16,512]{2,1,0:T(8,128)(2,1)S(1)} copy-done((bf16[4,16,512]{2,1,0:T(8,128)(2,1)S(1)}, bf16[4,16,512]{2,1,0:T(8,128)(2,1)}, u32[]{:S(2)}) %copy-start.6) | copy-done | bytes 65560
  36.1 0.7 %copy-done.7 = f32[8,512]{1,0:T(8,128)S(1)} copy-done((f32[8,512]{1,0:T(8,128)S(1)}, f32[8,512]{1,0:T(8,128)}, u32[]{:S(2)}) %copy-start.7) | copy-done | bytes 16408
  36.9 0.0 copy-start.8
  36.9 0.7 %copy-done.8 = bf16[3,512]{1,0:T(4,128)(2,1)S(1)} copy-done((bf16[3,512]{1,0:T(4,128)(2,1)S(1)}, bf16[3,512]{1,0:T(4,128)(2,1)}, u32[]{:S(2)}) %copy-start.8) | copy-done | bytes 3096
  37.6 0.0 copy-start
  37.6 0.0 copy-start.4
  37.6 0.0 copy-start.5
  37.6 1.8 %own_half.1 = (f32[3,48,512]{2,1,0:T(8,128)S(1)}, bf16[256,768]{1,0:T(8,128)(2,1)S(1)}) custom-call(bf16[512,128]{1,0:T(8,128)(2,1)S(1)} %bitcast.5, bf16[64,512]{1,0:T(8,128)(2,1)S(1)} %bitcast.6, f32[8,512]{1,0:T(8,128)S(1)} %copy-done.7, bf16[3,512]{1,0:T(4,128)(2,1)S(1)} %copy-done.8, bf16[512,512]{1,0:T(8,128)(2,1)S(1)} %copy-done.1, ...), custom_call_target="tpu_custom_call" | custom-call | flops 4000000000 | bytes 2000000 | tf_op jit(solution)/shard_map/own_half/pallas_call | solution.py:237
  39.4 0.0 collective-permute-done
  39.4 0.0 copy-done
  39.4 0.0 copy-done.4
  39.4 0.0 copy-done.5
  39.4 0.0 copy-done.9
  39.4 3.4 %window.1 = bf16[3,6,12,512]{3,2,1,0:T(8,128)(2,1)} custom-call(bf16[256,128]{1,0:T(8,128)(2,1)S(1)} %bitcast.7, f32[3,48,512]{2,1,0:T(8,128)S(1)} %get-tuple-element.7.own_ref, bf16[256,768]{1,0:T(8,128)(2,1)S(1)} %get-tuple-element.8.folded_ref, bf16[3,512]{1,0:T(4,128)(2,1)S(1)} %copy-done.9, bf16[512,512]{1,0:T(8,128)(2,1)S(1)} %copy-done.4, ...), custom_call_target="tpu_custom_call" | custom-call | flops 8000000000 | bytes 4000000 | tf_op jit(solution)/shard_map/window/pallas_call | solution.py:257
  (4 shorter events, 0.0 us)
Async XLA Ops:
  26.9 12.5 %collective-permute-start = (bf16[32,8,128]{2,1,0:T(8,128)(2,1)S(1)}, bf16[32,8,128]{2,1,0:T(8,128)(2,1)S(1)}, u32[]{:S(2)}, u32[]{:S(2)}) collective-permute-start(bf16[32,8,128]{2,1,0:T(8,128)(2,1)S(1)} %slice.4), channel_id=1, source_target_pairs={{0,15},{1,0},{2,1},{3,2},{4,3},{5,4},{6,5},{7,6},{8,7},{9,8},{10,9... | collective-permute-start | bytes 196616 | tf_op jit(solution)/shard_map/ppermute | solution.py:235
  32.2 1.0 %copy-start.1 = (bf16[512,512]{1,0:T(8,128)(2,1)S(1)}, bf16[512,512]{1,0:T(8,128)(2,1)}, u32[]{:S(2)}) copy-start(bf16[512,512]{1,0:T(8,128)(2,1)} %key_ref.1) | copy-start | bytes 1572868
  33.2 1.0 %copy-start.2 = (bf16[512,512]{1,0:T(8,128)(2,1)S(1)}, bf16[512,512]{1,0:T(8,128)(2,1)}, u32[]{:S(2)}) copy-start(bf16[512,512]{1,0:T(8,128)(2,1)} %value_ref.1) | copy-start | bytes 1572868
  34.3 1.0 %copy-start.3 = (bf16[512,512]{1,0:T(8,128)(2,1)S(1)}, bf16[512,512]{1,0:T(8,128)(2,1)}, u32[]{:S(2)}) copy-start(bf16[512,512]{1,0:T(8,128)(2,1)} %out_w_ref.3) | copy-start | bytes 1572868
  35.3 0.8 %copy-start.6 = (bf16[4,16,512]{2,1,0:T(8,128)(2,1)S(1)}, bf16[4,16,512]{2,1,0:T(8,128)(2,1)}, u32[]{:S(2)}) copy-start(bf16[4,16,512]{2,1,0:T(8,128)(2,1)} %param.10) | copy-start | bytes 196612
  36.1 0.7 %copy-start.7 = (f32[8,512]{1,0:T(8,128)S(1)}, f32[8,512]{1,0:T(8,128)}, u32[]{:S(2)}) copy-start(f32[8,512]{1,0:T(8,128)} %level_ref.1) | copy-start | bytes 49156
  36.9 0.7 %copy-start.8 = (bf16[3,512]{1,0:T(4,128)(2,1)S(1)}, bf16[3,512]{1,0:T(4,128)(2,1)}, u32[]{:S(2)}) copy-start(bf16[3,512]{1,0:T(4,128)(2,1)} %query_ref.3) | copy-start | bytes 9220
  37.6 1.8 %copy-start = (bf16[512,1536]{1,0:T(8,128)(2,1)S(1)}, bf16[512,1536]{1,0:T(8,128)(2,1)}, u32[]{:S(2)}) copy-start(bf16[512,1536]{1,0:T(8,128)(2,1)} %qkv_w_ref.1) | copy-start | bytes 4718596
  37.6 1.8 %copy-start.4 = (bf16[512,512]{1,0:T(8,128)(2,1)S(1)}, bf16[512,512]{1,0:T(8,128)(2,1)}, u32[]{:S(2)}) copy-start(bf16[512,512]{1,0:T(8,128)(2,1)} %out_w_ref.3) | copy-start | bytes 1572868
  37.6 1.8 %copy-start.5 = (bf16[512,512]{1,0:T(8,128)(2,1)S(1)}, bf16[512,512]{1,0:T(8,128)(2,1)}, u32[]{:S(2)}) copy-start(bf16[512,512]{1,0:T(8,128)(2,1)} %proj_w_ref.1) | copy-start | bytes 1572868
  37.6 1.8 %copy-start.9 = (bf16[3,512]{1,0:T(4,128)(2,1)S(1)}, bf16[3,512]{1,0:T(4,128)(2,1)}, u32[]{:S(2)}) copy-start(bf16[3,512]{1,0:T(4,128)(2,1)} %query_ref.3) | copy-start | bytes 9220

commit v2 on v1

--- a/solution.py
+++ b/solution.py
@@ -36,27 +36,32 @@
     return high, value - high
 
 
-def pack_kernel(pixel_ref, out_ref, rows):
-    count, cols = pixel_ref.shape
+def pack_kernel(pixel_ref, out_ref, placed):
+    cols, count = pixel_ref.shape
     band = PATCH * WLAT
     bands = count // band
-    rows[pl.ds(0, count), pl.ds(0, cols)] = pixel_ref[...].astype(F32)
-    rows[pl.ds(count, 16), :] = jnp.zeros((16, LANES), F32)
     source, target = iota((cols, 2 * LANES), 0), iota((cols, 2 * LANES), 1)
-    base = source // (cols // 2) * LANES + source % (cols // 2)
-    total = None
-    for r in range(PATCH):
-        picked = jnp.concatenate(
-            [rows[pl.ds(band * g + r, SLOT, stride=PATCH), :] for g in range(bands)], axis=0
-        )[:, :cols].astype(BF16)
-        place = jnp.where(target == base + r * GROUP, 1.0, 0.0).astype(BF16)
-        part = mul(picked, place)
-        total = part if total is None else total + part
-    west = total[:, :LANES].reshape(bands, SLOT, LANES)
-    own = total[:, LANES:].reshape(bands, SLOT, LANES)
-    out_ref[...] = (
-        jnp.concatenate([west, own], axis=1).reshape(bands * 2 * SLOT, LANES).astype(BF16)
-    )
+    place = (target // LANES == source // (cols // 2)) & (target % GROUP == source % (cols // 2))
+    wide = lax.dot_general(
+        pixel_ref[...],
+        jnp.where(place, 1.0, 0.0).astype(BF16),
+        (((0,), (0,)), ((), ())),
+        preferred_element_type=F32,
+    )
+    for h in range(2):
+        placed[h, pl.ds(0, count), :] = wide[:, h * LANES : (h + 1) * LANES]
+        placed[h, pl.ds(count, 16), :] = jnp.zeros((16, LANES), F32)
+    turn = iota((1, LANES), 1) // GROUP
+    for g in range(bands):
+        halves = []
+        for h in range(2):
+            block = placed[h, pl.ds(band * g, SLOT, stride=PATCH), :]
+            for r in range(1, PATCH):
+                block = jnp.where(
+                    turn == r, placed[h, pl.ds(band * g + r, SLOT, stride=PATCH), :], block
+                )
+            halves.append(block)
+        out_ref[pl.ds(g * 2 * SLOT, 2 * SLOT), :] = jnp.concatenate(halves, axis=0).astype(BF16)
 
 
 def fold_weights(embed_ref, level_ref, query_ref, key_ref, value_ref):
@@ -225,15 +230,18 @@
         out_shape=jax.ShapeDtypeStruct((bands * 2 * SLOT, LANES), BF16),
         in_specs=whole(1),
         out_specs=whole(1)[0],
-        scratch_shapes=[pltpu.VMEM((count + 16, LANES), F32)],
+        scratch_shapes=[pltpu.VMEM((2, count + 16, LANES), F32)],
+        compiler_params=pltpu.CompilerParams(vmem_limit_bytes=8 * 2**20),
+        cost_estimate=pl.CostEstimate(flops=8 * 10**9, bytes_accessed=2 * 10**5, transcendentals=0),
         name="pack",
-    )(pixels[0])
+    )(pixels[0].T)
     block = lax.all_to_all(
         packed.reshape(bands, 2 * SLOT, LANES), "var", split_axis=0, concat_axis=0, tiled=True
     )
     sectors = lax.axis_size("lon")
     east = lax.ppermute(block[:, :SLOT], "lon", [(i, (i - 1) % sectors) for i in range(sectors)])
     fields = block.shape[0]
+    weights = (embed_weight.reshape(-1, width), level_code, queries, w_key, w_value, w_out)
     own, folded = pl.pallas_call(
         own_kernel,
         out_shape=[
@@ -246,13 +254,7 @@
         cost_estimate=pl.CostEstimate(flops=4 * 10**9, bytes_accessed=2 * 10**6, transcendentals=0),
         name="own_half",
     )(
-        block.reshape(fields * 2 * SLOT, LANES),
-        embed_weight.reshape(-1, width),
-        level_code,
-        queries,
-        w_key,
-        w_value,
-        w_out,
+        block.reshape(fields * 2 * SLOT, LANES), *weights
     )
     return pl.pallas_call(
         window_kernel,

time: 43.3 us -> 37.9 us (0.88)
  the two profiles are of different devices: /device:TPU:8 before, /device:TPU:1 now
where the time goes in v2:
time: 37.9 us; the launch traced here: 37.7 us
  blocking collectives  23.6 us (62%)
  Pallas kernels  5.51 us (15%)
  starting transfers between devices  4 us (11%)
  waiting for transfers between devices  3.59 us (9%)
  local copies, waits for them, and re-layouts  0.93 us (2%)
    all_to_all x1, blocking collectives, body(): lax.all_to_all(packed.reshape(bands, 2 * SLOT, LANES), 'var', split_axis=...  23.6 us
    ppermute x1, starting transfers between devices, body(): lax.ppermute(block[:, :SLOT], 'lon', [(i, (i - 1) % sectors) for i in ran...  4 us
    ppermute x1, waiting for transfers between devices, body(): lax.ppermute(block[:, :SLOT], 'lon', [(i, (i - 1) % sectors) for i in ran...  3.59 us
    pallas_call x1, Pallas kernels, body(): pl.pallas_call(window_kernel, out_shape=jax.ShapeDtypeStruct((LATENT, WLA...  3.42 us
    pallas_call x1, Pallas kernels, body(): pl.pallas_call(own_kernel, out_shape=[jax.ShapeDtypeStruct((LATENT, HALF...  1.79 us
    unnamed x18, local copies, waits for them, and re-layouts  0.92 us
  transfers between devices with their start and end apart: 1, of which 1 were waited for; matrix products, arithmetic and copies ran while one was open for 0% of the time, Pallas kernels for 5%

profile of v2, /device:TPU:1, one launch (start us, length us, event | category | flops | bytes accessed | tf_op | source)
XLA Modules:
  0.0 37.7 jit_solution(2900088012706985605)
XLA Ops:
  0.0 0.0 copy-start.5
  0.0 0.9 %copy-done.5 = bf16[1,768,48]{1,2,0:T(8,128)(2,1)S(1)} copy-done((bf16[1,768,48]{1,2,0:T(8,128)(2,1)S(1)}, bf16[1,768,48]{1,2,0:T(8,128)(2,1)}, u32[]{:S(2)}) %copy-start.5) | copy-done | bytes 73752
  0.9 0.0 copy-start.1
  0.9 0.0 copy-start.2
  0.9 0.0 copy-start.3
  0.9 0.0 copy-start.6
  0.9 0.0 copy-start.7
  0.9 0.0 copy-start.8
  0.9 0.3 pack.1
  1.2 23.6 %all_to_all.5 = bf16[32,16,128]{2,1,0:T(8,128)(2,1)S(1)} all-to-all(bf16[32,16,128]{2,1,0:T(8,128)(2,1)S(1)} %bitcast.8), channel_id=1, replica_groups=mesh['var'=32,'lon'=16] {'var'}, dimensions={0} | all-to-all | bytes 262144 | tf_op jit(solution)/shard_map/all_to_all | solution.py:238
  24.8 4.0 %collective-permute-start = (bf16[32,8,128]{2,1,0:T(8,128)(2,1)S(1)}, bf16[32,8,128]{2,1,0:T(8,128)(2,1)S(1)}, u32[]{:S(2)}, u32[]{:S(2)}) collective-permute-start(bf16[32,8,128]{2,1,0:T(8,128)(2,1)S(1)} %slice.4), channel_id=1, source_target_pairs={{0,15},{1,0},{2,1},{3,2},{4,3},{5,4},{6,5},{7,6},{8,7},{9,8},{10,9... | collective-permute-start | bytes 196616 | tf_op jit(solution)/shard_map/ppermute | solution.py:242
  28.8 0.0 copy-done.1
  28.8 0.0 copy-done.2
  28.8 0.0 copy-done.3
  28.8 0.0 copy-done.6
  28.9 0.0 copy-done.7
  28.9 0.0 copy-done.8
  28.9 0.0 copy-start
  28.9 0.0 copy-start.4
  28.9 1.8 %own_half.1 = (f32[3,48,512]{2,1,0:T(8,128)S(1)}, bf16[256,768]{1,0:T(8,128)(2,1)S(1)}) custom-call(bf16[512,128]{1,0:T(8,128)(2,1)S(1)} %bitcast.7, bf16[64,512]{1,0:T(8,128)(2,1)S(1)} %bitcast.10, f32[8,512]{1,0:T(8,128)S(1)} %copy-done.7, bf16[3,512]{1,0:T(4,128)(2,1)S(1)} %copy-done.8, bf16[512,512]{1,0:T(8,128)(2,1)S(1)} %copy-done.1, ...), custom_call_target="tpu_custom_call" | custom-call | flops 4000000000 | bytes 2000000 | tf_op jit(solution)/shard_map/own_half/pallas_call | solution.py:245
  30.7 3.6 %collective-permute-done = bf16[32,8,128]{2,1,0:T(8,128)(2,1)S(1)} collective-permute-done((bf16[32,8,128]{2,1,0:T(8,128)(2,1)S(1)}, bf16[32,8,128]{2,1,0:T(8,128)(2,1)S(1)}, u32[]{:S(2)}, u32[]{:S(2)}) %collective-permute-start) | collective-permute-done | bytes 65568 | tf_op jit(solution)/shard_map/ppermute | solution.py:242
  34.3 0.0 copy-done
  34.3 0.0 copy-done.4
  34.3 3.4 %window.1 = bf16[3,6,12,512]{3,2,1,0:T(8,128)(2,1)} custom-call(bf16[256,128]{1,0:T(8,128)(2,1)S(1)} %bitcast.11, f32[3,48,512]{2,1,0:T(8,128)S(1)} %get-tuple-element.7.own_ref, bf16[256,768]{1,0:T(8,128)(2,1)S(1)} %get-tuple-element.8.folded_ref, bf16[3,512]{1,0:T(4,128)(2,1)S(1)} %copy-done.8, bf16[512,512]{1,0:T(8,128)(2,1)S(1)} %copy-done.3, ...), custom_call_target="tpu_custom_call" | custom-call | flops 8000000000 | bytes 4000000 | tf_op jit(solution)/shard_map/window/pallas_call | solution.py:259
  (1 shorter events, 0.0 us)
Async XLA Ops:
  0.0 0.9 %copy-start.5 = (bf16[1,768,48]{1,2,0:T(8,128)(2,1)S(1)}, bf16[1,768,48]{1,2,0:T(8,128)(2,1)}, u32[]{:S(2)}) copy-start(bf16[1,768,48]{1,2,0:T(8,128)(2,1)} %param.9) | copy-start | bytes 221188
  0.9 27.9 %copy-start.1 = (bf16[512,512]{1,0:T(8,128)(2,1)S(1)}, bf16[512,512]{1,0:T(8,128)(2,1)}, u32[]{:S(2)}) copy-start(bf16[512,512]{1,0:T(8,128)(2,1)} %key_ref.1) | copy-start | bytes 1572868
  0.9 27.9 %copy-start.2 = (bf16[512,512]{1,0:T(8,128)(2,1)S(1)}, bf16[512,512]{1,0:T(8,128)(2,1)}, u32[]{:S(2)}) copy-start(bf16[512,512]{1,0:T(8,128)(2,1)} %value_ref.1) | copy-start | bytes 1572868
  0.9 27.9 %copy-start.3 = (bf16[512,512]{1,0:T(8,128)(2,1)S(1)}, bf16[512,512]{1,0:T(8,128)(2,1)}, u32[]{:S(2)}) copy-start(bf16[512,512]{1,0:T(8,128)(2,1)} %out_w_ref.3) | copy-start | bytes 1572868
  0.9 28.0 %copy-start.6 = (bf16[4,16,512]{2,1,0:T(8,128)(2,1)S(1)}, bf16[4,16,512]{2,1,0:T(8,128)(2,1)}, u32[]{:S(2)}) copy-start(bf16[4,16,512]{2,1,0:T(8,128)(2,1)} %param.10) | copy-start | bytes 196612
  0.9 28.0 %copy-start.7 = (f32[8,512]{1,0:T(8,128)S(1)}, f32[8,512]{1,0:T(8,128)}, u32[]{:S(2)}) copy-start(f32[8,512]{1,0:T(8,128)} %level_ref.1) | copy-start | bytes 49156
  0.9 28.0 %copy-start.8 = (bf16[3,512]{1,0:T(4,128)(2,1)S(1)}, bf16[3,512]{1,0:T(4,128)(2,1)}, u32[]{:S(2)}) copy-start(bf16[3,512]{1,0:T(4,128)(2,1)} %query_ref.3) | copy-start | bytes 9220
  24.8 9.5 %collective-permute-start = (bf16[32,8,128]{2,1,0:T(8,128)(2,1)S(1)}, bf16[32,8,128]{2,1,0:T(8,128)(2,1)S(1)}, u32[]{:S(2)}, u32[]{:S(2)}) collective-permute-start(bf16[32,8,128]{2,1,0:T(8,128)(2,1)S(1)} %slice.4), channel_id=1, source_target_pairs={{0,15},{1,0},{2,1},{3,2},{4,3},{5,4},{6,5},{7,6},{8,7},{9,8},{10,9... | collective-permute-start | bytes 196616 | tf_op jit(solution)/shard_map/ppermute | solution.py:242
  28.9 5.4 %copy-start = (bf16[512,1536]{1,0:T(8,128)(2,1)S(1)}, bf16[512,1536]{1,0:T(8,128)(2,1)}, u32[]{:S(2)}) copy-start(bf16[512,1536]{1,0:T(8,128)(2,1)} %qkv_w_ref.1) | copy-start | bytes 4718596
  28.9 5.4 %copy-start.4 = (bf16[512,512]{1,0:T(8,128)(2,1)S(1)}, bf16[512,512]{1,0:T(8,128)(2,1)}, u32[]{:S(2)}) copy-start(bf16[512,512]{1,0:T(8,128)(2,1)} %proj_w_ref.1) | copy-start | bytes 1572868

commit v3 on v2

--- a/solution.py
+++ b/solution.py
@@ -52,13 +52,17 @@
         placed[h, pl.ds(0, count), :] = wide[:, h * LANES : (h + 1) * LANES]
         placed[h, pl.ds(count, 16), :] = jnp.zeros((16, LANES), F32)
     turn = iota((1, LANES), 1) // GROUP
+    far = (1 - lax.axis_index("lon") % 2) * (count // 2)
     for g in range(bands):
         halves = []
         for h in range(2):
-            block = placed[h, pl.ds(band * g, SLOT, stride=PATCH), :]
+            base = band * g
+            if h == 0:
+                base = pl.multiple_of(far + base if g < bands // 2 else base - far, SLOT)
+            block = placed[h, pl.ds(base, SLOT, stride=PATCH), :]
             for r in range(1, PATCH):
                 block = jnp.where(
-                    turn == r, placed[h, pl.ds(band * g + r, SLOT, stride=PATCH), :], block
+                    turn == r, placed[h, pl.ds(base + r, SLOT, stride=PATCH), :], block
                 )
             halves.append(block)
         out_ref[pl.ds(g * 2 * SLOT, 2 * SLOT), :] = jnp.concatenate(halves, axis=0).astype(BF16)
@@ -221,11 +225,10 @@
     return [pl.BlockSpec(memory_space=pltpu.VMEM)] * count
 
 
-def body(pixels, embed_weight, level_code, queries, w_key, w_value, w_out, w_qkv, w_proj):
-    _, count, cols = pixels.shape
+def pack(pixels):
+    _, count, _ = pixels.shape
     bands = count // (PATCH * WLAT)
-    width = w_out.shape[0]
-    packed = pl.pallas_call(
+    return pl.pallas_call(
         pack_kernel,
         out_shape=jax.ShapeDtypeStruct((bands * 2 * SLOT, LANES), BF16),
         in_specs=whole(1),
@@ -235,14 +238,11 @@
         cost_estimate=pl.CostEstimate(flops=8 * 10**9, bytes_accessed=2 * 10**5, transcendentals=0),
         name="pack",
     )(pixels[0].T)
-    block = lax.all_to_all(
-        packed.reshape(bands, 2 * SLOT, LANES), "var", split_axis=0, concat_axis=0, tiled=True
-    )
-    sectors = lax.axis_size("lon")
-    east = lax.ppermute(block[:, :SLOT], "lon", [(i, (i - 1) % sectors) for i in range(sectors)])
-    fields = block.shape[0]
-    weights = (embed_weight.reshape(-1, width), level_code, queries, w_key, w_value, w_out)
-    own, folded = pl.pallas_call(
+
+
+def own_half(block, embed_weight, level_code, queries, w_key, w_value, w_out):
+    width = w_out.shape[0]
+    return pl.pallas_call(
         own_kernel,
         out_shape=[
             jax.ShapeDtypeStruct((LATENT, HALF * SLOT, width), F32),
@@ -253,9 +253,11 @@
         compiler_params=pltpu.CompilerParams(vmem_limit_bytes=24 * 2**20),
         cost_estimate=pl.CostEstimate(flops=4 * 10**9, bytes_accessed=2 * 10**6, transcendentals=0),
         name="own_half",
-    )(
-        block.reshape(fields * 2 * SLOT, LANES), *weights
-    )
+    )(block.reshape(-1, LANES), embed_weight.reshape(-1, width), level_code, queries, w_key, w_value, w_out)
+
+
+def window(east, own, folded, queries, w_out, w_qkv, w_proj):
+    width = w_out.shape[0]
     return pl.pallas_call(
         window_kernel,
         out_shape=jax.ShapeDtypeStruct((LATENT, WLAT, WLON, width), BF16),
@@ -268,7 +270,27 @@
         compiler_params=pltpu.CompilerParams(vmem_limit_bytes=32 * 2**20),
         cost_estimate=pl.CostEstimate(flops=8 * 10**9, bytes_accessed=4 * 10**6, transcendentals=0),
         name="window",
-    )(east.reshape(fields * SLOT, LANES), own, folded, queries, w_out, w_qkv, w_proj)
+    )(east.reshape(-1, LANES), own, folded, queries, w_out, w_qkv, w_proj)
+
+
+def western_pairs(bands, sectors):
+    pairs = []
+    for g in range(bands):
+        for l in range(sectors):
+            source = (g + l % 2 * (bands // 2)) % bands
+            pairs.append((source * sectors + (l + 1) % sectors, g * sectors + l))
+    return pairs
+
+
+def body(pixels, embed_weight, level_code, queries, w_key, w_value, w_out, w_qkv, w_proj):
+    packed = pack(pixels)
+    bands, sectors = lax.axis_size("var"), lax.axis_size("lon")
+    block = lax.all_to_all(
+        packed.reshape(bands, 2 * SLOT, LANES), "var", split_axis=0, concat_axis=0, tiled=True
+    )
+    east = lax.ppermute(block[:, :SLOT], ("var", "lon"), western_pairs(bands, sectors))
+    own, folded = own_half(block, embed_weight, level_code, queries, w_key, w_value, w_out)
+    return window(east, own, folded, queries, w_out, w_qkv, w_proj)
 
 
 def solution(mesh):

time: 37.9 us -> 36.1 us (0.953)
  waiting for transfers between devices: 3.59 us -> 1.8 us
    ppermute x1, waiting for transfers between devices: 3.59 us -> 1.8 us  [body(): lax.ppermute(block[:, :SLOT], ('var', 'lon'), western_pairs(bands, sectors))]
where the time goes in v3:
time: 36.1 us; the launch traced here: 35.9 us
  blocking collectives  23.6 us (65%)
  Pallas kernels  5.54 us (15%)
  starting transfers between devices  4 us (11%)
  waiting for transfers between devices  1.8 us (5%)
  local copies, waits for them, and re-layouts  0.93 us (3%)
    all_to_all x1, blocking collectives, body(): lax.all_to_all(packed.reshape(bands, 2 * SLOT, LANES), 'var', split_axis=...  23.6 us
    ppermute x1, starting transfers between devices, body(): lax.ppermute(block[:, :SLOT], ('var', 'lon'), western_pairs(bands, sectors))  4 us
    pallas_call x1, Pallas kernels, window(): pl.pallas_call(window_kernel, out_shape=jax.ShapeDtypeStruct((LATENT, WLA...  3.41 us
    ppermute x1, waiting for transfers between devices, body(): lax.ppermute(block[:, :SLOT], ('var', 'lon'), western_pairs(bands, sectors))  1.8 us
    pallas_call x1, Pallas kernels, own_half(): pl.pallas_call(own_kernel, out_shape=[jax.ShapeDtypeStruct((LATENT, HALF...  1.79 us
    unnamed x18, local copies, waits for them, and re-layouts  0.92 us
  transfers between devices with their start and end apart: 1, of which 1 were waited for; matrix products, arithmetic and copies ran while one was open for 0% of the time, Pallas kernels for 5%

profile of v3, /device:TPU:1, one launch (start us, length us, event | category | flops | bytes accessed | tf_op | source)
XLA Modules:
  0.0 35.9 jit_solution(17826838737158973856)
XLA Ops:
  0.0 0.0 copy-start.5
  0.0 0.9 %copy-done.5 = bf16[1,768,48]{1,2,0:T(8,128)(2,1)S(1)} copy-done((bf16[1,768,48]{1,2,0:T(8,128)(2,1)S(1)}, bf16[1,768,48]{1,2,0:T(8,128)(2,1)}, u32[]{:S(2)}) %copy-start.5) | copy-done | bytes 73752
  0.9 0.0 copy-start.1
  0.9 0.0 copy-start.2
  0.9 0.0 copy-start.3
  0.9 0.0 copy-start.6
  0.9 0.0 copy-start.7
  0.9 0.0 copy-start.8
  0.9 0.3 pack.1
  1.3 23.6 %all_to_all.5 = bf16[32,16,128]{2,1,0:T(8,128)(2,1)S(1)} all-to-all(bf16[32,16,128]{2,1,0:T(8,128)(2,1)S(1)} %bitcast.8), channel_id=1, replica_groups=mesh['var'=32,'lon'=16] {'var'}, dimensions={0} | all-to-all | bytes 262144 | tf_op jit(solution)/shard_map/all_to_all | solution.py:288
  24.8 4.0 %collective-permute-start = (bf16[32,8,128]{2,1,0:T(8,128)(2,1)S(1)}, bf16[32,8,128]{2,1,0:T(8,128)(2,1)S(1)}, u32[]{:S(2)}, u32[]{:S(2)}) collective-permute-start(bf16[32,8,128]{2,1,0:T(8,128)(2,1)S(1)} %slice.4), channel_id=1, source_target_pairs={{1,0},{258,1},{3,2},{260,3},{5,4},{262,5},{7,6},{264,7},{9,8},{266... | collective-permute-start | bytes 196616 | tf_op jit(solution)/shard_map/ppermute | solution.py:291
  28.9 0.0 copy-done.1
  28.9 0.0 copy-done.2
  28.9 0.0 copy-done.3
  28.9 0.0 copy-done.6
  28.9 0.0 copy-done.7
  28.9 0.0 copy-done.8
  28.9 0.0 copy-start
  28.9 0.0 copy-start.4
  28.9 1.8 %own_half.1 = (f32[3,48,512]{2,1,0:T(8,128)S(1)}, bf16[256,768]{1,0:T(8,128)(2,1)S(1)}) custom-call(bf16[512,128]{1,0:T(8,128)(2,1)S(1)} %bitcast.7, bf16[64,512]{1,0:T(8,128)(2,1)S(1)} %bitcast.10, f32[8,512]{1,0:T(8,128)S(1)} %copy-done.7, bf16[3,512]{1,0:T(4,128)(2,1)S(1)} %copy-done.8, bf16[512,512]{1,0:T(8,128)(2,1)S(1)} %copy-done.1, ...), custom_call_target="tpu_custom_call" | custom-call | flops 4000000000 | bytes 2000000 | tf_op jit(solution)/shard_map/own_half/pallas_call | solution.py:245
  30.7 1.8 %collective-permute-done = bf16[32,8,128]{2,1,0:T(8,128)(2,1)S(1)} collective-permute-done((bf16[32,8,128]{2,1,0:T(8,128)(2,1)S(1)}, bf16[32,8,128]{2,1,0:T(8,128)(2,1)S(1)}, u32[]{:S(2)}, u32[]{:S(2)}) %collective-permute-start) | collective-permute-done | bytes 65568 | tf_op jit(solution)/shard_map/ppermute | solution.py:291
  32.5 0.0 copy-done
  32.5 0.0 copy-done.4
  32.5 3.4 %window.1 = bf16[3,6,12,512]{3,2,1,0:T(8,128)(2,1)} custom-call(bf16[256,128]{1,0:T(8,128)(2,1)S(1)} %bitcast.11, f32[3,48,512]{2,1,0:T(8,128)S(1)} %get-tuple-element.7.own_ref, bf16[256,768]{1,0:T(8,128)(2,1)S(1)} %get-tuple-element.8.folded_ref, bf16[3,512]{1,0:T(4,128)(2,1)S(1)} %copy-done.8, bf16[512,512]{1,0:T(8,128)(2,1)S(1)} %copy-done.3, ...), custom_call_target="tpu_custom_call" | custom-call | flops 8000000000 | bytes 4000000 | tf_op jit(solution)/shard_map/window/pallas_call | solution.py:261
  (1 shorter events, 0.0 us)
Async XLA Ops:
  0.0 0.9 %copy-start.5 = (bf16[1,768,48]{1,2,0:T(8,128)(2,1)S(1)}, bf16[1,768,48]{1,2,0:T(8,128)(2,1)}, u32[]{:S(2)}) copy-start(bf16[1,768,48]{1,2,0:T(8,128)(2,1)} %param.9) | copy-start | bytes 221188
  0.9 28.0 %copy-start.1 = (bf16[512,512]{1,0:T(8,128)(2,1)S(1)}, bf16[512,512]{1,0:T(8,128)(2,1)}, u32[]{:S(2)}) copy-start(bf16[512,512]{1,0:T(8,128)(2,1)} %key_ref.1) | copy-start | bytes 1572868
  0.9 28.0 %copy-start.2 = (bf16[512,512]{1,0:T(8,128)(2,1)S(1)}, bf16[512,512]{1,0:T(8,128)(2,1)}, u32[]{:S(2)}) copy-start(bf16[512,512]{1,0:T(8,128)(2,1)} %value_ref.1) | copy-start | bytes 1572868
  0.9 28.0 %copy-start.3 = (bf16[512,512]{1,0:T(8,128)(2,1)S(1)}, bf16[512,512]{1,0:T(8,128)(2,1)}, u32[]{:S(2)}) copy-start(bf16[512,512]{1,0:T(8,128)(2,1)} %out_w_ref.3) | copy-start | bytes 1572868
  0.9 28.0 %copy-start.6 = (bf16[4,16,512]{2,1,0:T(8,128)(2,1)S(1)}, bf16[4,16,512]{2,1,0:T(8,128)(2,1)}, u32[]{:S(2)}) copy-start(bf16[4,16,512]{2,1,0:T(8,128)(2,1)} %param.10) | copy-start | bytes 196612
  0.9 28.0 %copy-start.7 = (f32[8,512]{1,0:T(8,128)S(1)}, f32[8,512]{1,0:T(8,128)}, u32[]{:S(2)}) copy-start(f32[8,512]{1,0:T(8,128)} %level_ref.1) | copy-start | bytes 49156
  0.9 28.0 %copy-start.8 = (bf16[3,512]{1,0:T(4,128)(2,1)S(1)}, bf16[3,512]{1,0:T(4,128)(2,1)}, u32[]{:S(2)}) copy-start(bf16[3,512]{1,0:T(4,128)(2,1)} %query_ref.3) | copy-start | bytes 9220
  24.8 7.7 %collective-permute-start = (bf16[32,8,128]{2,1,0:T(8,128)(2,1)S(1)}, bf16[32,8,128]{2,1,0:T(8,128)(2,1)S(1)}, u32[]{:S(2)}, u32[]{:S(2)}) collective-permute-start(bf16[32,8,128]{2,1,0:T(8,128)(2,1)S(1)} %slice.4), channel_id=1, source_target_pairs={{1,0},{258,1},{3,2},{260,3},{5,4},{262,5},{7,6},{264,7},{9,8},{266... | collective-permute-start | bytes 196616 | tf_op jit(solution)/shard_map/ppermute | solution.py:291
  28.9 3.6 %copy-start = (bf16[512,1536]{1,0:T(8,128)(2,1)S(1)}, bf16[512,1536]{1,0:T(8,128)(2,1)}, u32[]{:S(2)}) copy-start(bf16[512,1536]{1,0:T(8,128)(2,1)} %qkv_w_ref.1) | copy-start | bytes 4718596
  28.9 3.6 %copy-start.4 = (bf16[512,512]{1,0:T(8,128)(2,1)S(1)}, bf16[512,512]{1,0:T(8,128)(2,1)}, u32[]{:S(2)}) copy-start(bf16[512,512]{1,0:T(8,128)(2,1)} %proj_w_ref.1) | copy-start | bytes 1572868

commit v4 on v3

v4 whole, which is shorter than its diff:
```python
import jax
import jax.numpy as jnp
from jax import lax
from jax.experimental import pallas as pl
from jax.experimental.pallas import tpu as pltpu
from jax.sharding import PartitionSpec as P

HEAD = 64
LATENT = 3
WLAT = 6
WLON = 12
HALF = WLON // 2
PATCH = 4
SLOT = 8
LANES = 128
GROUP = 32
HALF_ROWS = 112
LOG2E = 1.4426950408889634
F32 = jnp.float32
BF16 = jnp.bfloat16


def mul(a, b):
    return jnp.dot(a, b, preferred_element_type=F32)


def mul_t(a, b):
    return lax.dot_general(a, b, (((1,), (1,)), ((), ())), preferred_element_type=F32)


def iota(shape, dim):
    return lax.broadcasted_iota(jnp.int32, shape, dim)


def split(value):
    high = value.astype(BF16).astype(F32)
    return high, value - high


def pack_kernel(pixel_ref, out_ref, placed):
    cols, count = pixel_ref.shape
    band = PATCH * WLAT
    bands = count // band
    source, target = iota((cols, 2 * LANES), 0), iota((cols, 2 * LANES), 1)
    place = (target // LANES == source // (cols // 2)) & (target % GROUP == source % (cols // 2))
    wide = lax.dot_general(
        pixel_ref[...],
        jnp.where(place, 1.0, 0.0).astype(BF16),
        (((0,), (0,)), ((), ())),
        preferred_element_type=F32,
    )
    for h in range(2):
        placed[h, pl.ds(0, count), :] = wide[:, h * LANES : (h + 1) * LANES]
        placed[h, pl.ds(count, 16), :] = jnp.zeros((16, LANES), F32)
    turn = iota((1, LANES), 1) // GROUP
    far = (1 - lax.axis_index("lon") % 2) * (count // 2)
    for g in range(bands):
        halves = []
        for h in range(2):
            base = band * g
            if h == 0:
                base = pl.multiple_of(far + base if g < bands // 2 else base - far, SLOT)
            block = placed[h, pl.ds(base, SLOT, stride=PATCH), :]
            for r in range(1, PATCH):
                block = jnp.where(
                    turn == r, placed[h, pl.ds(base + r, SLOT, stride=PATCH), :], block
                )
            halves.append(block)
        out_ref[pl.ds(g * 2 * SLOT, 2 * SLOT), :] = jnp.concatenate(halves, axis=0).astype(BF16)


def fold_weights(embed_ref, level_ref, query_ref, key_ref, value_ref):
    pixels, width = embed_ref.shape
    levels = level_ref.shape[0]
    ext = jnp.concatenate([embed_ref[...].astype(F32), level_ref[...]], axis=0)
    count = pixels + levels
    ext = ext - jnp.mean(ext, axis=-1, keepdims=True)
    high, low = split(ext)
    stacked = jnp.concatenate([high, low], axis=0).astype(BF16)
    keys = mul(stacked, key_ref[...])
    keys = keys[:count] + keys[count:]
    values = mul(stacked, value_ref[...])
    values = values[:count] + values[count:]
    heads = width // HEAD
    scores = None
    for q in range(LATENT):
        high_q, low_q = split(keys * query_ref[pl.ds(q, 1), :].astype(F32))
        both = jnp.concatenate([high_q, low_q], axis=0).astype(BF16)
        collect = jnp.where(
            iota((width, LANES), 1) == q * heads + iota((width, LANES), 0) // HEAD, 1.0, 0.0
        ).astype(BF16)
        part = mul(both, collect)
        part = part[:count] + part[count:]
        scores = part if scores is None else scores + part
    scores = scores * (HEAD ** (-0.5) * LOG2E)
    zeros = jnp.zeros((LANES - count, width), F32)
    high_t = jnp.concatenate([high, zeros], axis=0).astype(BF16)
    low_t = jnp.concatenate([low, zeros], axis=0).astype(BF16)
    high_b, low_b = high.astype(BF16), low.astype(BF16)
    gram = (mul_t(high_b, high_t) + (mul_t(high_b, low_t) + mul_t(low_b, high_t))) * (1.0 / width)
    row, lane = iota((count, LANES), 0), iota((count, LANES), 1)
    diagonal = jnp.sum(jnp.where(row == lane, gram, 0.0), axis=-1, keepdims=True)
    spread = jnp.where(row < pixels, gram, 2.0 * gram)
    spread = jnp.where(
        lane < pixels, spread, jnp.where((lane == pixels) & (row >= pixels), diagonal, 0.0)
    )
    folded = jnp.concatenate([spread, scores, values], axis=1)
    high_f, low_f = split(folded)
    rest = jnp.zeros((2 * LANES - 2 * count, folded.shape[1]), F32)
    return jnp.concatenate(
        [high_f[:pixels], low_f[:pixels], high_f[pixels:], low_f[pixels:], rest], axis=0
    ).astype(BF16)


def constants(fields, levels, width):
    variables = fields // levels
    pixels = variables * PATCH * PATCH
    heads = width // HEAD
    depth = variables * LANES
    source, target = iota((depth, LANES), 0), iota((depth, LANES), 1)
    place = (
        source // LANES * (PATCH * PATCH) + source % LANES // GROUP * PATCH + source % PATCH
    )
    column = source % GROUP // PATCH
    gather = jnp.concatenate(
        [jnp.where((target % pixels == place) & (column == b), 1.0, 0.0) for b in range(HALF)],
        axis=1,
    ).astype(BF16)
    count = HALF * levels * SLOT
    row, lane = iota((count, LANES), 0), iota((count, LANES), 1)
    level = jnp.where(
        (lane < 2 * levels) & (lane % levels == row // SLOT % levels), 1.0, 0.0
    ).astype(BF16)
    spread = jnp.concatenate(
        [
            jnp.where(
                iota((LANES, width), 0) == q * heads + iota((LANES, width), 1) // HEAD, 1.0, 0.0
            )
            for q in range(LATENT)
        ],
        axis=1,
    ).astype(BF16)
    return gather, level, spread


def aggregate_half(rows, folded, gather, level, spread, query_ref, out_weight):
    count = level.shape[0]
    levels = count // (HALF * SLOT)
    variables = rows.shape[0] // levels
    width = out_weight.shape[0]
    pixels = variables * PATCH * PATCH
    grid = rows.reshape(levels, variables, SLOT, LANES)
    wide = jnp.concatenate(
        [grid[:, v].reshape(levels * SLOT, LANES) for v in range(variables)], axis=1
    ).astype(BF16)
    lane = iota((1, LANES), 1)
    parts = 2
    each = HALF // parts
    size = each * levels * SLOT
    patch = mul(wide, gather)
    stage = []
    for k in range(parts):
        part = jnp.concatenate(
            [patch[:, b * LANES : (b + 1) * LANES] for b in range(k * each, (k + 1) * each)], axis=0
        )
        full = jnp.concatenate([part.astype(BF16), level[:size]], axis=1)
        stage.append((part, full, mul(full, folded[:, : 2 * LANES])))
    ready = []
    for part, full, product in stage:
        moment, scores = product[:, :LANES], product[:, LANES:]
        values = mul(full, folded[:, 2 * LANES :])
        variance = jnp.sum(jnp.where(lane == pixels, 1.0, part) * moment, axis=-1, keepdims=True)
        scale = lax.rsqrt(jnp.maximum(variance, 0.0) + 1e-05)
        expo = jnp.exp2(scores * scale).reshape(each, levels, SLOT, LANES)
        weights = expo / jnp.sum(expo, axis=1, keepdims=True) * scale.reshape(each, levels, SLOT, 1)
        ready.append((weights.reshape(size, LANES).astype(BF16), values))
    pieces = [[] for _ in range(LATENT)]
    for weights, values in ready:
        for q in range(LATENT):
            part = mul(weights, spread[:, q * width : (q + 1) * width]) * values
            pieces[q].append(part.reshape(each, levels, SLOT, width).sum(axis=1).reshape(each * SLOT, width))
    mixed = [jnp.concatenate(p, axis=0) for p in pieces]
    attended = jnp.concatenate(mixed, axis=0).astype(BF16)
    latent = mul(attended, out_weight).reshape(LATENT, HALF * SLOT, width)
    latent = latent + query_ref[...].astype(F32)[:, None, :]
    return latent.astype(BF16).astype(F32)


def tokens_of(latent, slots, clean, qkv_weight):
    width = latent.shape[-1]
    for c in range(width // LANES):
        slots[c] = latent[:, :, c * LANES : (c + 1) * LANES].reshape(slots.shape[1:])
    pairs = LATENT * WLAT
    for q in range(LATENT):
        for a in range(WLAT):
            for c in range(width // LANES):
                clean[pl.ds((q * WLAT + a) * HALF, HALF), pl.ds(c * LANES, LANES)] = slots[
                    c, pl.ds(q * HALF * SLOT + a, HALF, stride=SLOT), :
                ]
    clean[pl.ds(pairs * HALF, HALF_ROWS - pairs * HALF), :] = jnp.zeros(
        (HALF_ROWS - pairs * HALF, width), F32
    )
    shifted = clean[...]
    center = shifted - jnp.mean(shifted, axis=-1, keepdims=True)
    spread = jnp.mean(center * center, axis=-1, keepdims=True)
    normed = (center * lax.rsqrt(spread + 1e-05)).astype(BF16)
    return shifted, mul(normed, qkv_weight).astype(BF16)


def own_kernel(
    block_ref, embed_ref, level_ref, query_ref, key_ref, value_ref, out_w_ref, qkv_w_ref,
    shifted_ref, qkv_ref, folded_ref, gather_ref, marks_ref, spread_ref, slots, clean,
):
    folded = fold_weights(embed_ref, level_ref, query_ref, key_ref, value_ref)
    folded_ref[...] = folded
    fields = block_ref.shape[0] // (2 * SLOT)
    gather, marks, spread = constants(fields, level_ref.shape[0], out_w_ref.shape[0])
    gather_ref[...] = gather
    marks_ref[...] = marks
    spread_ref[...] = spread
    rows = block_ref[...].astype(F32).reshape(fields, 2, SLOT, LANES)[:, 1]
    latent = aggregate_half(rows, folded, gather, marks, spread, query_ref, out_w_ref[...])
    shifted, qkv = tokens_of(latent, slots, clean, qkv_w_ref[...])
    shifted_ref[...] = shifted
    qkv_ref[...] = qkv


def window_kernel(
    block_ref, shifted_ref, qkv_ref, folded_ref, gather_ref, marks_ref, spread_ref, query_ref,
    out_w_ref, qkv_w_ref, proj_w_ref, out_ref, slots, clean, result,
):
    fields = block_ref.shape[0] // SLOT
    width = out_w_ref.shape[0]
    rows = block_ref[...].astype(F32).reshape(fields, SLOT, LANES)
    latent = aggregate_half(
        rows, folded_ref[...], gather_ref[...], marks_ref[...], spread_ref[...], query_ref, out_w_ref[...]
    )
    shifted, qkv = tokens_of(latent, slots, clean, qkv_w_ref[...])
    shifted = jnp.concatenate([shifted_ref[...], shifted], axis=0)
    qkv = jnp.concatenate([qkv_ref[...], qkv], axis=0)
    pairs = LATENT * WLAT
    row = iota((2 * HALF_ROWS, LANES), 0) % HALF_ROWS
    ones = jnp.where(row < pairs * HALF, 1.0, 0.0).astype(BF16)
    first = iota((1, LANES), 1) < HEAD
    mixed = []
    alls = []
    for p in range(width // LANES):
        queries = qkv[:, p * LANES : (p + 1) * LANES]
        keys = qkv[:, width + p * LANES : width + (p + 1) * LANES]
        values = qkv[:, 2 * width + p * LANES : 2 * width + (p + 1) * LANES]
        values = jnp.concatenate([values * BF16(2.0**-8), ones], axis=1)
        zero = jnp.zeros_like(queries)
        chosen = jnp.concatenate([jnp.where(first, queries, zero), jnp.where(first, zero, queries)], axis=0)
        scores = mul_t(chosen, keys)
        alls.append((jnp.exp2(scores * (HEAD ** (-0.5) * LOG2E)).astype(BF16), values))
    for expo, values in alls:
        found = mul(expo, values).reshape(2, 2 * HALF_ROWS, 2 * LANES)
        both = jnp.where(jnp.concatenate([first, first], axis=1), found[0], found[1])
        mixed.append((both[:, :LANES] / both[:, LANES:] * 2.0**8).astype(BF16))
    result[...] = shifted + mul(jnp.concatenate(mixed, axis=1), proj_w_ref[...])
    for i in range(pairs):
        out_ref[i // WLAT, i % WLAT] = jnp.concatenate(
            [result[pl.ds(i * HALF, HALF), :], result[pl.ds(HALF_ROWS + i * HALF, HALF), :]], axis=0
        ).astype(BF16)


def whole(count):
    return [pl.BlockSpec(memory_space=pltpu.VMEM)] * count


def pack(pixels):
    _, count, _ = pixels.shape
    bands = count // (PATCH * WLAT)
    return pl.pallas_call(
        pack_kernel,
        out_shape=jax.ShapeDtypeStruct((bands * 2 * SLOT, LANES), BF16),
        in_specs=whole(1),
        out_specs=whole(1)[0],
        scratch_shapes=[pltpu.VMEM((2, count + 16, LANES), F32)],
        compiler_params=pltpu.CompilerParams(vmem_limit_bytes=8 * 2**20),
        cost_estimate=pl.CostEstimate(flops=8 * 10**9, bytes_accessed=2 * 10**5, transcendentals=0),
        name="pack",
    )(pixels[0].T)


def scratch(width):
    return [
        pltpu.VMEM((width // LANES, LATENT * HALF * SLOT, LANES), F32),
        pltpu.VMEM((HALF_ROWS, width), F32),
    ]


def own_half(block, embed_weight, level_code, queries, w_key, w_value, w_out, w_qkv):
    width = w_out.shape[0]
    fields, levels = block.shape[0], level_code.shape[0]
    return pl.pallas_call(
        own_kernel,
        out_shape=[
            jax.ShapeDtypeStruct((HALF_ROWS, width), F32),
            jax.ShapeDtypeStruct((HALF_ROWS, w_qkv.shape[1]), BF16),
            jax.ShapeDtypeStruct((2 * LANES, width + 2 * LANES), BF16),
            jax.ShapeDtypeStruct((fields // levels * LANES, HALF * LANES), BF16),
            jax.ShapeDtypeStruct((HALF * levels * SLOT, LANES), BF16),
            jax.ShapeDtypeStruct((LANES, LATENT * width), BF16),
        ],
        in_specs=whole(8),
        out_specs=whole(6),
        scratch_shapes=scratch(width),
        compiler_params=pltpu.CompilerParams(vmem_limit_bytes=24 * 2**20),
        cost_estimate=pl.CostEstimate(flops=4 * 10**9, bytes_accessed=2 * 10**6, transcendentals=0),
        name="own_half",
    )(
        block.reshape(-1, LANES), embed_weight.reshape(-1, width), level_code, queries, w_key, w_value,
        w_out, w_qkv,
    )


def window(east, own, queries, w_out, w_qkv, w_proj):
    width = w_out.shape[0]
    return pl.pallas_call(
        window_kernel,
        out_shape=jax.ShapeDtypeStruct((LATENT, WLAT, WLON, width), BF16),
        in_specs=whole(11),
        out_specs=whole(1)[0],
        scratch_shapes=scratch(width) + [pltpu.VMEM((2 * HALF_ROWS, width), F32)],
        compiler_params=pltpu.CompilerParams(vmem_limit_bytes=32 * 2**20),
        cost_estimate=pl.CostEstimate(flops=8 * 10**9, bytes_accessed=4 * 10**6, transcendentals=0),
        name="window",
    )(east.reshape(-1, LANES), *own, queries, w_out, w_qkv, w_proj)


def western_pairs(bands, sectors):
    pairs = []
    for g in range(bands):
        for l in range(sectors):
            source = (g + l % 2 * (bands // 2)) % bands
            pairs.append((source * sectors + (l + 1) % sectors, g * sectors + l))
    return pairs


def body(pixels, embed_weight, level_code, queries, w_key, w_value, w_out, w_qkv, w_proj):
    packed = pack(pixels)
    bands, sectors = lax.axis_size("var"), lax.axis_size("lon")
    block = lax.all_to_all(
        packed.reshape(bands, 2 * SLOT, LANES), "var", split_axis=0, concat_axis=0, tiled=True
    )
    east = lax.ppermute(block[:, :SLOT], ("var", "lon"), western_pairs(bands, sectors))
    own = own_half(block, embed_weight, level_code, queries, w_key, w_value, w_out, w_qkv)
    return window(east, own, queries, w_out, w_qkv, w_proj)


def solution(mesh):
    placed = (P("var", None, "lon"), P(), P(), P(), P(), P(), P(), P(), P())
    return jax.shard_map(
        body, mesh=mesh, in_specs=placed, out_specs=P(None, "var", "lon", None), check_vma=False
    )
```

time: 36.1 us -> 35.8 us (level)
  waiting for transfers between devices: 1.8 us -> 1.24 us
    pallas_call x1, Pallas kernels: 1.79 us -> 2.34 us  [own_half(): pl.pallas_call(own_kernel, out_shape=[jax.ShapeDtypeStruct((HALF_ROWS, wi...]
    ppermute x1, waiting for transfers between devices: 1.8 us -> 1.24 us  [body(): lax.ppermute(block[:, :SLOT], ('var', 'lon'), western_pairs(bands, sectors))]
  transfers between devices with their start and end apart: 1 -> 1, of which waited for: 1 -> 1; matrix products, arithmetic and copies ran while one was open for 0% -> 0% of each run, Pallas kernels for 5% -> 7%
where the time goes in v4:
time: 35.8 us; the launch traced here: 35.7 us
  blocking collectives  23.6 us (66%)
  Pallas kernels  5.81 us (16%)
  starting transfers between devices  4 us (11%)
  waiting for transfers between devices  1.24 us (3%)
  local copies, waits for them, and re-layouts  0.92 us (3%)
    all_to_all x1, blocking collectives, body(): lax.all_to_all(packed.reshape(bands, 2 * SLOT, LANES), 'var', split_axis=...  23.6 us
    ppermute x1, starting transfers between devices, body(): lax.ppermute(block[:, :SLOT], ('var', 'lon'), western_pairs(bands, sectors))  4 us
    pallas_call x1, Pallas kernels, window(): pl.pallas_call(window_kernel, out_shape=jax.ShapeDtypeStruct((LATENT, WLA...  3.12 us
    pallas_call x1, Pallas kernels, own_half(): pl.pallas_call(own_kernel, out_shape=[jax.ShapeDtypeStruct((HALF_ROWS, wi...  2.34 us
    ppermute x1, waiting for transfers between devices, body(): lax.ppermute(block[:, :SLOT], ('var', 'lon'), western_pairs(bands, sectors))  1.24 us
    unnamed x18, local copies, waits for them, and re-layouts  0.92 us
  transfers between devices with their start and end apart: 1, of which 1 were waited for; matrix products, arithmetic and copies ran while one was open for 0% of the time, Pallas kernels for 7%

profile of v4, /device:TPU:1, one launch (start us, length us, event | category | flops | bytes accessed | tf_op | source)
XLA Modules:
  0.0 35.7 jit_solution(6450272233073142113)
XLA Ops:
  0.0 0.0 copy-start.5
  0.0 0.9 %copy-done.5 = bf16[1,768,48]{1,2,0:T(8,128)(2,1)S(1)} copy-done((bf16[1,768,48]{1,2,0:T(8,128)(2,1)S(1)}, bf16[1,768,48]{1,2,0:T(8,128)(2,1)}, u32[]{:S(2)}) %copy-start.5) | copy-done | bytes 73752
  0.9 0.0 copy-start
  0.9 0.0 copy-start.1
  0.9 0.0 copy-start.2
  0.9 0.0 copy-start.3
  0.9 0.0 copy-start.6
  0.9 0.0 copy-start.7
  0.9 0.0 copy-start.8
  0.9 0.3 pack.1
  1.3 23.6 %all_to_all.5 = bf16[32,16,128]{2,1,0:T(8,128)(2,1)S(1)} all-to-all(bf16[32,16,128]{2,1,0:T(8,128)(2,1)S(1)} %bitcast.8), channel_id=1, replica_groups=mesh['var'=32,'lon'=16] {'var'}, dimensions={0} | all-to-all | bytes 262144 | tf_op jit(solution)/shard_map/all_to_all | solution.py:344
  24.9 4.0 %collective-permute-start = (bf16[32,8,128]{2,1,0:T(8,128)(2,1)S(1)}, bf16[32,8,128]{2,1,0:T(8,128)(2,1)S(1)}, u32[]{:S(2)}, u32[]{:S(2)}) collective-permute-start(bf16[32,8,128]{2,1,0:T(8,128)(2,1)S(1)} %slice.4), channel_id=1, source_target_pairs={{1,0},{258,1},{3,2},{260,3},{5,4},{262,5},{7,6},{264,7},{9,8},{266... | collective-permute-start | bytes 196616 | tf_op jit(solution)/shard_map/ppermute | solution.py:347
  28.9 0.0 copy-done
  28.9 0.0 copy-done.1
  28.9 0.0 copy-done.2
  28.9 0.0 copy-done.3
  28.9 0.0 copy-done.6
  28.9 0.0 copy-done.7
  28.9 0.0 copy-done.8
  28.9 0.0 copy-start.4
  28.9 2.3 %own_half.1 = (f32[112,512]{1,0:T(8,128)S(1)}, bf16[112,1536]{1,0:T(8,128)(2,1)S(1)}, bf16[256,768]{1,0:T(8,128)(2,1)S(1)}, bf16[512,768]{1,0:T(8,128)(2,1)S(1)}...) custom-call(bf16[512,128]{1,0:T(8,128)(2,1)S(1)} %bitcast.7, bf16[64,512]{1,0:T(8,128)(2,1)S(1)} %bitcast.10, ...), custom_call_target="tpu_custom_call" | custom-call | flops 4000000000 | bytes 2000000 | tf_op jit(solution)/shard_map/own_half/pallas_call | solution.py:296
  31.3 1.2 %collective-permute-done = bf16[32,8,128]{2,1,0:T(8,128)(2,1)S(1)} collective-permute-done((bf16[32,8,128]{2,1,0:T(8,128)(2,1)S(1)}, bf16[32,8,128]{2,1,0:T(8,128)(2,1)S(1)}, u32[]{:S(2)}, u32[]{:S(2)}) %collective-permute-start) | collective-permute-done | bytes 65568 | tf_op jit(solution)/shard_map/ppermute | solution.py:347
  32.5 0.0 copy-done.4
  32.5 3.1 %window.1 = bf16[3,6,12,512]{3,2,1,0:T(8,128)(2,1)} custom-call(bf16[256,128]{1,0:T(8,128)(2,1)S(1)} %bitcast.11, f32[112,512]{1,0:T(8,128)S(1)} %get-tuple-element.11.shifted_ref, bf16[112,1536]{1,0:T(8,128)(2,1)S(1)} %get-tuple-element.12.qkv_ref, bf16[256,768]{1,0:T(8,128)(2,1)S(1)} %get-tuple-element.13.folded_ref, ...), custom_call_target="tpu_custom_call" | custom-call | flops 8000000000 | bytes 4000000 | tf_op jit(solution)/shard_map/window/pallas_call | solution.py:320
  (1 shorter events, 0.0 us)
Async XLA Ops:
  0.0 0.9 %copy-start.5 = (bf16[1,768,48]{1,2,0:T(8,128)(2,1)S(1)}, bf16[1,768,48]{1,2,0:T(8,128)(2,1)}, u32[]{:S(2)}) copy-start(bf16[1,768,48]{1,2,0:T(8,128)(2,1)} %param.9) | copy-start | bytes 221188
  0.9 28.0 %copy-start = (bf16[512,1536]{1,0:T(8,128)(2,1)S(1)}, bf16[512,1536]{1,0:T(8,128)(2,1)}, u32[]{:S(2)}) copy-start(bf16[512,1536]{1,0:T(8,128)(2,1)} %qkv_w_ref.3) | copy-start | bytes 4718596
  0.9 28.0 %copy-start.1 = (bf16[512,512]{1,0:T(8,128)(2,1)S(1)}, bf16[512,512]{1,0:T(8,128)(2,1)}, u32[]{:S(2)}) copy-start(bf16[512,512]{1,0:T(8,128)(2,1)} %key_ref.1) | copy-start | bytes 1572868
  0.9 28.0 %copy-start.2 = (bf16[512,512]{1,0:T(8,128)(2,1)S(1)}, bf16[512,512]{1,0:T(8,128)(2,1)}, u32[]{:S(2)}) copy-start(bf16[512,512]{1,0:T(8,128)(2,1)} %value_ref.1) | copy-start | bytes 1572868
  0.9 28.0 %copy-start.3 = (bf16[512,512]{1,0:T(8,128)(2,1)S(1)}, bf16[512,512]{1,0:T(8,128)(2,1)}, u32[]{:S(2)}) copy-start(bf16[512,512]{1,0:T(8,128)(2,1)} %out_w_ref.3) | copy-start | bytes 1572868
  0.9 28.0 %copy-start.6 = (bf16[4,16,512]{2,1,0:T(8,128)(2,1)S(1)}, bf16[4,16,512]{2,1,0:T(8,128)(2,1)}, u32[]{:S(2)}) copy-start(bf16[4,16,512]{2,1,0:T(8,128)(2,1)} %param.10) | copy-start | bytes 196612
  0.9 28.0 %copy-start.7 = (f32[8,512]{1,0:T(8,128)S(1)}, f32[8,512]{1,0:T(8,128)}, u32[]{:S(2)}) copy-start(f32[8,512]{1,0:T(8,128)} %level_ref.1) | copy-start | bytes 49156
  0.9 28.0 %copy-start.8 = (bf16[3,512]{1,0:T(4,128)(2,1)S(1)}, bf16[3,512]{1,0:T(4,128)(2,1)}, u32[]{:S(2)}) copy-start(bf16[3,512]{1,0:T(4,128)(2,1)} %query_ref.3) | copy-start | bytes 9220
  24.9 7.7 %collective-permute-start = (bf16[32,8,128]{2,1,0:T(8,128)(2,1)S(1)}, bf16[32,8,128]{2,1,0:T(8,128)(2,1)S(1)}, u32[]{:S(2)}, u32[]{:S(2)}) collective-permute-start(bf16[32,8,128]{2,1,0:T(8,128)(2,1)S(1)} %slice.4), channel_id=1, source_target_pairs={{1,0},{258,1},{3,2},{260,3},{5,4},{262,5},{7,6},{264,7},{9,8},{266... | collective-permute-start | bytes 196616 | tf_op jit(solution)/shard_map/ppermute | solution.py:347
  28.9 3.6 %copy-start.4 = (bf16[512,512]{1,0:T(8,128)(2,1)S(1)}, bf16[512,512]{1,0:T(8,128)(2,1)}, u32[]{:S(2)}) copy-start(bf16[512,512]{1,0:T(8,128)(2,1)} %proj_w_ref.1) | copy-start | bytes 1572868

commit v5 on v4

--- a/solution.py
+++ b/solution.py
@@ -143,11 +143,11 @@
     return gather, level, spread
 
 
-def aggregate_half(rows, folded, gather, level, spread, query_ref, out_weight):
+def aggregate_half(rows, folded, gather, level, spread):
     count = level.shape[0]
     levels = count // (HALF * SLOT)
     variables = rows.shape[0] // levels
-    width = out_weight.shape[0]
+    width = spread.shape[1] // LATENT
     pixels = variables * PATCH * PATCH
     grid = rows.reshape(levels, variables, SLOT, LANES)
     wide = jnp.concatenate(
@@ -180,16 +180,33 @@
             part = mul(weights, spread[:, q * width : (q + 1) * width]) * values
             pieces[q].append(part.reshape(each, levels, SLOT, width).sum(axis=1).reshape(each * SLOT, width))
     mixed = [jnp.concatenate(p, axis=0) for p in pieces]
-    attended = jnp.concatenate(mixed, axis=0).astype(BF16)
-    latent = mul(attended, out_weight).reshape(LATENT, HALF * SLOT, width)
-    latent = latent + query_ref[...].astype(F32)[:, None, :]
-    return latent.astype(BF16).astype(F32)
-
-
-def tokens_of(latent, slots, clean, qkv_weight):
-    width = latent.shape[-1]
+    return jnp.concatenate(mixed, axis=0)
+
+
+def fold_window(query_ref, out_weight, qkv_weight):
+    weight = out_weight.astype(F32)
+    weight = weight - jnp.mean(weight, axis=-1, keepdims=True)
+    through = mul(weight.astype(BF16), qkv_weight).astype(BF16)
+    queries = query_ref[...].astype(F32)
+    high, low = split(queries - jnp.mean(queries, axis=-1, keepdims=True))
+    rest = jnp.zeros((16 - 2 * LATENT, queries.shape[1]), F32)
+    base = mul(jnp.concatenate([high, low, rest], axis=0).astype(BF16), qkv_weight)
+    base = base[:LATENT] + base[LATENT : 2 * LATENT]
+
+    def by_token(value):
+        latent = iota((HALF_ROWS, value.shape[1]), 0) // (WLAT * HALF)
+        rows = jnp.zeros(latent.shape, F32)
+        for q in range(LATENT):
+            rows = jnp.where(latent == q, value[q : q + 1], rows)
+        return rows
+
+    return through, by_token(base), by_token(queries)
+
+
+def tokens_of(attended, slots, clean, out_weight, through, base, queries):
+    width = attended.shape[1]
     for c in range(width // LANES):
-        slots[c] = latent[:, :, c * LANES : (c + 1) * LANES].reshape(slots.shape[1:])
+        slots[c] = attended[:, c * LANES : (c + 1) * LANES]
     pairs = LATENT * WLAT
     for q in range(LATENT):
         for a in range(WLAT):
@@ -200,16 +217,18 @@
     clean[pl.ds(pairs * HALF, HALF_ROWS - pairs * HALF), :] = jnp.zeros(
         (HALF_ROWS - pairs * HALF, width), F32
     )
-    shifted = clean[...]
+    tokens = clean[...].astype(BF16)
+    shifted = (mul(tokens, out_weight) + queries).astype(BF16).astype(F32)
+    qkv = mul(tokens, through) + base
     center = shifted - jnp.mean(shifted, axis=-1, keepdims=True)
     spread = jnp.mean(center * center, axis=-1, keepdims=True)
-    normed = (center * lax.rsqrt(spread + 1e-05)).astype(BF16)
-    return shifted, mul(normed, qkv_weight).astype(BF16)
+    return shifted, (qkv * lax.rsqrt(spread + 1e-05)).astype(BF16)
 
 
 def own_kernel(
     block_ref, embed_ref, level_ref, query_ref, key_ref, value_ref, out_w_ref, qkv_w_ref,
-    shifted_ref, qkv_ref, folded_ref, gather_ref, marks_ref, spread_ref, slots, clean,
+    shifted_ref, qkv_ref, folded_ref, gather_ref, marks_ref, spread_ref, through_ref, base_ref,
+    rows_ref, slots, clean,
 ):
     folded = fold_weights(embed_ref, level_ref, query_ref, key_ref, value_ref)
     folded_ref[...] = folded
@@ -218,24 +237,28 @@
     gather_ref[...] = gather
     marks_ref[...] = marks
     spread_ref[...] = spread
+    through, base, queries = fold_window(query_ref, out_w_ref[...], qkv_w_ref[...])
+    through_ref[...] = through
+    base_ref[...] = base
+    rows_ref[...] = queries
     rows = block_ref[...].astype(F32).reshape(fields, 2, SLOT, LANES)[:, 1]
-    latent = aggregate_half(rows, folded, gather, marks, spread, query_ref, out_w_ref[...])
-    shifted, qkv = tokens_of(latent, slots, clean, qkv_w_ref[...])
+    attended = aggregate_half(rows, folded, gather, marks, spread)
+    shifted, qkv = tokens_of(attended, slots, clean, out_w_ref[...], through, base, queries)
     shifted_ref[...] = shifted
     qkv_ref[...] = qkv
 
 
 def window_kernel(
-    block_ref, shifted_ref, qkv_ref, folded_ref, gather_ref, marks_ref, spread_ref, query_ref,
-    out_w_ref, qkv_w_ref, proj_w_ref, out_ref, slots, clean, result,
+    block_ref, shifted_ref, qkv_ref, folded_ref, gather_ref, marks_ref, spread_ref, through_ref,
+    base_ref, rows_ref, out_w_ref, proj_w_ref, out_ref, slots, clean, result,
 ):
     fields = block_ref.shape[0] // SLOT
     width = out_w_ref.shape[0]
     rows = block_ref[...].astype(F32).reshape(fields, SLOT, LANES)
-    latent = aggregate_half(
-        rows, folded_ref[...], gather_ref[...], marks_ref[...], spread_ref[...], query_ref, out_w_ref[...]
-    )
-    shifted, qkv = tokens_of(latent, slots, clean, qkv_w_ref[...])
+    attended = aggregate_half(rows, folded_ref[...], gather_ref[...], marks_ref[...], spread_ref[...])
+    shifted, qkv = tokens_of(
+        attended, slots, clean, out_w_ref[...], through_ref[...], base_ref[...], rows_ref[...]
+    )
     shifted = jnp.concatenate([shifted_ref[...], shifted], axis=0)
     qkv = jnp.concatenate([qkv_ref[...], qkv], axis=0)
     pairs = LATENT * WLAT
@@ -302,9 +325,12 @@
             jax.ShapeDtypeStruct((fields // levels * LANES, HALF * LANES), BF16),
             jax.ShapeDtypeStruct((HALF * levels * SLOT, LANES), BF16),
             jax.ShapeDtypeStruct((LANES, LATENT * width), BF16),
+            jax.ShapeDtypeStruct(w_qkv.shape, BF16),
+            jax.ShapeDtypeStruct((HALF_ROWS, w_qkv.shape[1]), F32),
+            jax.ShapeDtypeStruct((HALF_ROWS, width), F32),
         ],
         in_specs=whole(8),
-        out_specs=whole(6),
+        out_specs=whole(9),
         scratch_shapes=scratch(width),
         compiler_params=pltpu.CompilerParams(vmem_limit_bytes=24 * 2**20),
         cost_estimate=pl.CostEstimate(flops=4 * 10**9, bytes_accessed=2 * 10**6, transcendentals=0),
@@ -315,18 +341,18 @@
     )
 
 
-def window(east, own, queries, w_out, w_qkv, w_proj):
+def window(east, own, w_out, w_proj):
     width = w_out.shape[0]
     return pl.pallas_call(
         window_kernel,
         out_shape=jax.ShapeDtypeStruct((LATENT, WLAT, WLON, width), BF16),
-        in_specs=whole(11),
+        in_specs=whole(12),
         out_specs=whole(1)[0],
         scratch_shapes=scratch(width) + [pltpu.VMEM((2 * HALF_ROWS, width), F32)],
         compiler_params=pltpu.CompilerParams(vmem_limit_bytes=32 * 2**20),
         cost_estimate=pl.CostEstimate(flops=8 * 10**9, bytes_accessed=4 * 10**6, transcendentals=0),
         name="window",
-    )(east.reshape(-1, LANES), *own, queries, w_out, w_qkv, w_proj)
+    )(east.reshape(-1, LANES), *own, w_out, w_proj)
 
 
 def western_pairs(bands, sectors):
@@ -346,7 +372,7 @@
     )
     east = lax.ppermute(block[:, :SLOT], ("var", "lon"), western_pairs(bands, sectors))
     own = own_half(block, embed_weight, level_code, queries, w_key, w_value, w_out, w_qkv)
-    return window(east, own, queries, w_out, w_qkv, w_proj)
+    return window(east, own, w_out, w_proj)
 
 
 def solution(mesh):

time: 35.8 us -> 35.6 us (level)
  waiting for transfers between devices: 1.24 us -> 0.39 us
  Pallas kernels: 5.81 us -> 6.39 us
    pallas_call x1, Pallas kernels: 2.34 us -> 3.2 us  [own_half(): pl.pallas_call(own_kernel, out_shape=[jax.ShapeDtypeStruct((HALF_ROWS, wi...]
    ppermute x1, waiting for transfers between devices: 1.24 us -> 0.39 us  [body(): lax.ppermute(block[:, :SLOT], ('var', 'lon'), western_pairs(bands, sectors))]
  transfers between devices with their start and end apart: 1 -> 1, of which waited for: 1 -> 1; matrix products, arithmetic and copies ran while one was open for 0% -> 0% of each run, Pallas kernels for 7% -> 9%
where the time goes in v5:
time: 35.6 us; the launch traced here: 35.4 us
  blocking collectives  23.6 us (66%)
  Pallas kernels  6.39 us (18%)
  starting transfers between devices  4 us (11%)
  local copies, waits for them, and re-layouts  0.92 us (3%)
  waiting for transfers between devices  0.39 us (1%)
    all_to_all x1, blocking collectives, body(): lax.all_to_all(packed.reshape(bands, 2 * SLOT, LANES), 'var', split_axis=...  23.6 us
    ppermute x1, starting transfers between devices, body(): lax.ppermute(block[:, :SLOT], ('var', 'lon'), western_pairs(bands, sectors))  4 us
    pallas_call x1, Pallas kernels, own_half(): pl.pallas_call(own_kernel, out_shape=[jax.ShapeDtypeStruct((HALF_ROWS, wi...  3.2 us
    pallas_call x1, Pallas kernels, window(): pl.pallas_call(window_kernel, out_shape=jax.ShapeDtypeStruct((LATENT, WLA...  2.84 us
    unnamed x18, local copies, waits for them, and re-layouts  0.92 us
  transfers between devices with their start and end apart: 1, of which 1 were waited for; matrix products, arithmetic and copies ran while one was open for 0% of the time, Pallas kernels for 9%

profile of v5, /device:TPU:1, one launch (start us, length us, event | category | flops | bytes accessed | tf_op | source)
XLA Modules:
  0.0 35.4 jit_solution(2914943437906876095)
XLA Ops:
  0.0 0.0 copy-start.5
  0.0 0.9 %copy-done.5 = bf16[1,768,48]{1,2,0:T(8,128)(2,1)S(1)} copy-done((bf16[1,768,48]{1,2,0:T(8,128)(2,1)S(1)}, bf16[1,768,48]{1,2,0:T(8,128)(2,1)}, u32[]{:S(2)}) %copy-start.5) | copy-done | bytes 73752
  0.9 0.0 copy-start
  0.9 0.0 copy-start.1
  0.9 0.0 copy-start.2
  0.9 0.0 copy-start.3
  0.9 0.0 copy-start.6
  0.9 0.0 copy-start.7
  0.9 0.0 copy-start.8
  0.9 0.3 pack.1
  1.3 23.6 %all_to_all.5 = bf16[32,16,128]{2,1,0:T(8,128)(2,1)S(1)} all-to-all(bf16[32,16,128]{2,1,0:T(8,128)(2,1)S(1)} %bitcast.8), channel_id=1, replica_groups=mesh['var'=32,'lon'=16] {'var'}, dimensions={0} | all-to-all | bytes 262144 | tf_op jit(solution)/shard_map/all_to_all | solution.py:370
  24.9 4.0 %collective-permute-start = (bf16[32,8,128]{2,1,0:T(8,128)(2,1)S(1)}, bf16[32,8,128]{2,1,0:T(8,128)(2,1)S(1)}, u32[]{:S(2)}, u32[]{:S(2)}) collective-permute-start(bf16[32,8,128]{2,1,0:T(8,128)(2,1)S(1)} %slice.4), channel_id=1, source_target_pairs={{1,0},{258,1},{3,2},{260,3},{5,4},{262,5},{7,6},{264,7},{9,8},{266... | collective-permute-start | bytes 196616 | tf_op jit(solution)/shard_map/ppermute | solution.py:373
  28.9 0.0 copy-done
  28.9 0.0 copy-done.1
  28.9 0.0 copy-done.2
  28.9 0.0 copy-done.3
  28.9 0.0 copy-done.6
  28.9 0.0 copy-done.7
  28.9 0.0 copy-done.8
  28.9 0.0 copy-start.4
  28.9 3.2 %own_half.1 = (f32[112,512]{1,0:T(8,128)S(1)}, bf16[112,1536]{1,0:T(8,128)(2,1)S(1)}, bf16[256,768]{1,0:T(8,128)(2,1)S(1)}, bf16[512,768]{1,0:T(8,128)(2,1)S(1)}...) custom-call(bf16[512,128]{1,0:T(8,128)(2,1)S(1)} %bitcast.7, ...), custom_call_target="tpu_custom_call" | custom-call | flops 4000000000 | bytes 2000000 | tf_op jit(solution)/shard_map/own_half/pallas_call | solution.py:319
  32.2 0.4 %collective-permute-done = bf16[32,8,128]{2,1,0:T(8,128)(2,1)S(1)} collective-permute-done((bf16[32,8,128]{2,1,0:T(8,128)(2,1)S(1)}, bf16[32,8,128]{2,1,0:T(8,128)(2,1)S(1)}, u32[]{:S(2)}, u32[]{:S(2)}) %collective-permute-start) | collective-permute-done | bytes 65568 | tf_op jit(solution)/shard_map/ppermute | solution.py:373
  32.5 0.0 copy-done.4
  32.5 2.8 %window.1 = bf16[3,6,12,512]{3,2,1,0:T(8,128)(2,1)} custom-call(bf16[256,128]{1,0:T(8,128)(2,1)S(1)} %bitcast.11, f32[112,512]{1,0:T(8,128)S(1)} %get-tuple-element.14.shifted_ref, bf16[112,1536]{1,0:T(8,128)(2,1)S(1)} %get-tuple-element.15.qkv_ref, bf16[256,768]{1,0:T(8,128)(2,1)S(1)} %get-tuple-element.16.folded_ref, ...), custom_call_target="tpu_custom_call" | custom-call | flops 8000000000 | bytes 4000000 | tf_op jit(solution)/shard_map/window/pallas_call | solution.py:346
  (1 shorter events, 0.0 us)
Async XLA Ops:
  0.0 0.9 %copy-start.5 = (bf16[1,768,48]{1,2,0:T(8,128)(2,1)S(1)}, bf16[1,768,48]{1,2,0:T(8,128)(2,1)}, u32[]{:S(2)}) copy-start(bf16[1,768,48]{1,2,0:T(8,128)(2,1)} %param.9) | copy-start | bytes 221188
  0.9 28.0 %copy-start = (bf16[512,1536]{1,0:T(8,128)(2,1)S(1)}, bf16[512,1536]{1,0:T(8,128)(2,1)}, u32[]{:S(2)}) copy-start(bf16[512,1536]{1,0:T(8,128)(2,1)} %qkv_w_ref.1) | copy-start | bytes 4718596
  0.9 28.0 %copy-start.1 = (bf16[512,512]{1,0:T(8,128)(2,1)S(1)}, bf16[512,512]{1,0:T(8,128)(2,1)}, u32[]{:S(2)}) copy-start(bf16[512,512]{1,0:T(8,128)(2,1)} %key_ref.1) | copy-start | bytes 1572868
  0.9 28.0 %copy-start.2 = (bf16[512,512]{1,0:T(8,128)(2,1)S(1)}, bf16[512,512]{1,0:T(8,128)(2,1)}, u32[]{:S(2)}) copy-start(bf16[512,512]{1,0:T(8,128)(2,1)} %value_ref.1) | copy-start | bytes 1572868
  0.9 28.0 %copy-start.3 = (bf16[512,512]{1,0:T(8,128)(2,1)S(1)}, bf16[512,512]{1,0:T(8,128)(2,1)}, u32[]{:S(2)}) copy-start(bf16[512,512]{1,0:T(8,128)(2,1)} %out_w_ref.3) | copy-start | bytes 1572868
  0.9 28.0 %copy-start.6 = (bf16[4,16,512]{2,1,0:T(8,128)(2,1)S(1)}, bf16[4,16,512]{2,1,0:T(8,128)(2,1)}, u32[]{:S(2)}) copy-start(bf16[4,16,512]{2,1,0:T(8,128)(2,1)} %param.10) | copy-start | bytes 196612
  0.9 28.0 %copy-start.7 = (f32[8,512]{1,0:T(8,128)S(1)}, f32[8,512]{1,0:T(8,128)}, u32[]{:S(2)}) copy-start(f32[8,512]{1,0:T(8,128)} %level_ref.1) | copy-start | bytes 49156
  0.9 28.0 %copy-start.8 = (bf16[3,512]{1,0:T(4,128)(2,1)S(1)}, bf16[3,512]{1,0:T(4,128)(2,1)}, u32[]{:S(2)}) copy-start(bf16[3,512]{1,0:T(4,128)(2,1)} %query_ref.1) | copy-start | bytes 9220
  24.9 7.7 %collective-permute-start = (bf16[32,8,128]{2,1,0:T(8,128)(2,1)S(1)}, bf16[32,8,128]{2,1,0:T(8,128)(2,1)S(1)}, u32[]{:S(2)}, u32[]{:S(2)}) collective-permute-start(bf16[32,8,128]{2,1,0:T(8,128)(2,1)S(1)} %slice.4), channel_id=1, source_target_pairs={{1,0},{258,1},{3,2},{260,3},{5,4},{262,5},{7,6},{264,7},{9,8},{266... | collective-permute-start | bytes 196616 | tf_op jit(solution)/shard_map/ppermute | solution.py:373
  28.9 3.6 %copy-start.4 = (bf16[512,512]{1,0:T(8,128)(2,1)S(1)}, bf16[512,512]{1,0:T(8,128)(2,1)}, u32[]{:S(2)}) copy-start(bf16[512,512]{1,0:T(8,128)(2,1)} %proj_w_ref.1) | copy-start | bytes 1572868

commit v6 on v5

--- a/solution.py
+++ b/solution.py
@@ -20,6 +20,16 @@
 BF16 = jnp.bfloat16
 
 
+def member_order(members, depth=8):
+    far = [g for g in reversed(range(members)) if g % depth >= depth // 2]
+    near = sorted(
+        (g for g in range(members) if g % depth < depth // 2), key=lambda g: (g % depth, g), reverse=True
+    )
+    first = far.index(members // 2 + depth - 2)
+    far[0], far[first] = far[first], far[0]
+    return [g for pair in zip(far, near) for g in pair]
+
+
 def mul(a, b):
     return jnp.dot(a, b, preferred_element_type=F32)
 
@@ -54,7 +64,7 @@
         placed[h, pl.ds(count, 16), :] = jnp.zeros((16, LANES), F32)
     turn = iota((1, LANES), 1) // GROUP
     far = (1 - lax.axis_index("lon") % 2) * (count // 2)
-    for g in range(bands):
+    for place_at, g in enumerate(member_order(bands)):
         halves = []
         for h in range(2):
             base = band * g
@@ -66,7 +76,7 @@
                     turn == r, placed[h, pl.ds(base + r, SLOT, stride=PATCH), :], block
                 )
             halves.append(block)
-        out_ref[pl.ds(g * 2 * SLOT, 2 * SLOT), :] = jnp.concatenate(halves, axis=0).astype(BF16)
+        out_ref[pl.ds(place_at * 2 * SLOT, 2 * SLOT), :] = jnp.concatenate(halves, axis=0).astype(BF16)
 
 
 def fold_weights(embed_ref, level_ref, query_ref, key_ref, value_ref):
@@ -149,9 +159,13 @@
     variables = rows.shape[0] // levels
     width = spread.shape[1] // LATENT
     pixels = variables * PATCH * PATCH
-    grid = rows.reshape(levels, variables, SLOT, LANES)
+    order = member_order(rows.shape[0])
     wide = jnp.concatenate(
-        [grid[:, v].reshape(levels * SLOT, LANES) for v in range(variables)], axis=1
+        [
+            jnp.concatenate([rows[order.index(l * variables + v)] for l in range(levels)], axis=0)
+            for v in range(variables)
+        ],
+        axis=1,
     ).astype(BF16)
     lane = iota((1, LANES), 1)
     parts = 2
@@ -368,7 +382,12 @@
     packed = pack(pixels)
     bands, sectors = lax.axis_size("var"), lax.axis_size("lon")
     block = lax.all_to_all(
-        packed.reshape(bands, 2 * SLOT, LANES), "var", split_axis=0, concat_axis=0, tiled=True
+        packed.reshape(bands, 2 * SLOT, LANES),
+        "var",
+        split_axis=0,
+        concat_axis=0,
+        axis_index_groups=[member_order(bands)],
+        tiled=True,
     )
     east = lax.ppermute(block[:, :SLOT], ("var", "lon"), western_pairs(bands, sectors))
     own = own_half(block, embed_weight, level_code, queries, w_key, w_value, w_out, w_qkv)

time: 35.6 us -> 34.3 us (0.963)
  the two profiles are of different devices: /device:TPU:1 before, /device:TPU:8 now
where the time goes in v6:
time: 34.3 us; the launch traced here: 34.1 us
  blocking collectives  19.8 us (58%)
  starting transfers between devices  6.89 us (20%)
  Pallas kernels  6.4 us (19%)
  local copies, waits for them, and re-layouts  0.92 us (3%)
    all_to_all x1, blocking collectives, body(): lax.all_to_all(packed.reshape(bands, 2 * SLOT, LANES), 'var', split_axis=...  19.8 us
    ppermute x1, starting transfers between devices, body(): lax.ppermute(block[:, :SLOT], ('var', 'lon'), western_pairs(bands, sectors))  6.89 us
    pallas_call x1, Pallas kernels, own_half(): pl.pallas_call(own_kernel, out_shape=[jax.ShapeDtypeStruct((HALF_ROWS, wi...  3.21 us
    pallas_call x1, Pallas kernels, window(): pl.pallas_call(window_kernel, out_shape=jax.ShapeDtypeStruct((LATENT, WLA...  2.84 us
    unnamed x18, local copies, waits for them, and re-layouts  0.92 us
  transfers between devices with their start and end apart: 1, of which 0 were waited for; matrix products, arithmetic and copies ran while one was open for 0% of the time, Pallas kernels for 9%

profile of v6, /device:TPU:8, one launch (start us, length us, event | category | flops | bytes accessed | tf_op | source)
XLA Modules:
  0.0 34.1 jit_solution(4213268656865323074)
XLA Ops:
  0.0 0.0 copy-start.5
  0.0 0.9 %copy-done.5 = bf16[1,768,48]{1,2,0:T(8,128)(2,1)S(1)} copy-done((bf16[1,768,48]{1,2,0:T(8,128)(2,1)S(1)}, bf16[1,768,48]{1,2,0:T(8,128)(2,1)}, u32[]{:S(2)}) %copy-start.5) | copy-done | bytes 73752
  0.9 0.0 copy-start
  0.9 0.0 copy-start.1
  0.9 0.0 copy-start.2
  0.9 0.0 copy-start.3
  0.9 0.0 copy-start.6
  0.9 0.0 copy-start.7
  0.9 0.0 copy-start.8
  0.9 0.3 %pack.1 = bf16[512,128]{1,0:T(8,128)(2,1)S(1)} custom-call(bf16[48,768]{1,0:T(8,128)(2,1)S(1)} %bitcast.9), custom_call_target="tpu_custom_call" | custom-call | flops 8000000000 | bytes 200000 | tf_op jit(solution)/shard_map/pack/pallas_call | solution.py:311
  1.3 19.8 %all_to_all.5 = bf16[32,16,128]{2,1,0:T(8,128)(2,1)S(1)} all-to-all(bf16[32,16,128]{2,1,0:T(8,128)(2,1)S(1)} %bitcast.8), channel_id=1, replica_groups={{352,432,480,304,464,176,448,48,368,416,496,288,336,160,320,32,240,400,..., dimensions={0} | all-to-all | bytes 262144 | tf_op jit(solution)/shard_map/all_to_all | solution.py:384
  21.0 6.9 %collective-permute-start = (bf16[32,8,128]{2,1,0:T(8,128)(2,1)S(1)}, bf16[32,8,128]{2,1,0:T(8,128)(2,1)S(1)}, u32[]{:S(2)}, u32[]{:S(2)}) collective-permute-start(bf16[32,8,128]{2,1,0:T(8,128)(2,1)S(1)} %slice.4), channel_id=1, source_target_pairs={{1,0},{258,1},{3,2},{260,3},{5,4},{262,5},{7,6},{264,7},{9,8},{266... | collective-permute-start | bytes 196616 | tf_op jit(solution)/shard_map/ppermute | solution.py:392
  27.9 0.0 copy-done
  27.9 0.0 copy-done.1
  28.0 0.0 copy-done.2
  28.0 0.0 copy-done.3
  28.0 0.0 copy-done.6
  28.0 0.0 copy-done.7
  28.0 0.0 copy-done.8
  28.0 0.0 copy-start.4
  28.0 3.2 %own_half.1 = (f32[112,512]{1,0:T(8,128)S(1)}, bf16[112,1536]{1,0:T(8,128)(2,1)S(1)}, bf16[256,768]{1,0:T(8,128)(2,1)S(1)}, bf16[512,768]{1,0:T(8,128)(2,1)S(1)}...) custom-call(bf16[512,128]{1,0:T(8,128)(2,1)S(1)} %bitcast.7, ...), custom_call_target="tpu_custom_call" | custom-call | flops 4000000000 | bytes 2000000 | tf_op jit(solution)/shard_map/own_half/pallas_call | solution.py:333
  31.2 0.0 collective-permute-done
  31.2 0.0 copy-done.4
  31.3 2.8 %window.1 = bf16[3,6,12,512]{3,2,1,0:T(8,128)(2,1)} custom-call(bf16[256,128]{1,0:T(8,128)(2,1)S(1)} %bitcast.11, f32[112,512]{1,0:T(8,128)S(1)} %get-tuple-element.14.shifted_ref, bf16[112,1536]{1,0:T(8,128)(2,1)S(1)} %get-tuple-element.15.qkv_ref, bf16[256,768]{1,0:T(8,128)(2,1)S(1)} %get-tuple-element.16.folded_ref, ...), custom_call_target="tpu_custom_call" | custom-call | flops 8000000000 | bytes 4000000 | tf_op jit(solution)/shard_map/window/pallas_call | solution.py:360
  (1 shorter events, 0.0 us)
Async XLA Ops:
  0.0 0.9 %copy-start.5 = (bf16[1,768,48]{1,2,0:T(8,128)(2,1)S(1)}, bf16[1,768,48]{1,2,0:T(8,128)(2,1)}, u32[]{:S(2)}) copy-start(bf16[1,768,48]{1,2,0:T(8,128)(2,1)} %param.9) | copy-start | bytes 221188
  0.9 27.1 %copy-start = (bf16[512,1536]{1,0:T(8,128)(2,1)S(1)}, bf16[512,1536]{1,0:T(8,128)(2,1)}, u32[]{:S(2)}) copy-start(bf16[512,1536]{1,0:T(8,128)(2,1)} %qkv_w_ref.1) | copy-start | bytes 4718596
  0.9 27.1 %copy-start.1 = (bf16[512,512]{1,0:T(8,128)(2,1)S(1)}, bf16[512,512]{1,0:T(8,128)(2,1)}, u32[]{:S(2)}) copy-start(bf16[512,512]{1,0:T(8,128)(2,1)} %key_ref.1) | copy-start | bytes 1572868
  0.9 27.1 %copy-start.2 = (bf16[512,512]{1,0:T(8,128)(2,1)S(1)}, bf16[512,512]{1,0:T(8,128)(2,1)}, u32[]{:S(2)}) copy-start(bf16[512,512]{1,0:T(8,128)(2,1)} %value_ref.1) | copy-start | bytes 1572868
  0.9 27.1 %copy-start.3 = (bf16[512,512]{1,0:T(8,128)(2,1)S(1)}, bf16[512,512]{1,0:T(8,128)(2,1)}, u32[]{:S(2)}) copy-start(bf16[512,512]{1,0:T(8,128)(2,1)} %out_w_ref.3) | copy-start | bytes 1572868
  0.9 27.1 %copy-start.6 = (bf16[4,16,512]{2,1,0:T(8,128)(2,1)S(1)}, bf16[4,16,512]{2,1,0:T(8,128)(2,1)}, u32[]{:S(2)}) copy-start(bf16[4,16,512]{2,1,0:T(8,128)(2,1)} %param.10) | copy-start | bytes 196612
  0.9 27.1 %copy-start.7 = (f32[8,512]{1,0:T(8,128)S(1)}, f32[8,512]{1,0:T(8,128)}, u32[]{:S(2)}) copy-start(f32[8,512]{1,0:T(8,128)} %level_ref.1) | copy-start | bytes 49156
  0.9 27.1 %copy-start.8 = (bf16[3,512]{1,0:T(4,128)(2,1)S(1)}, bf16[3,512]{1,0:T(4,128)(2,1)}, u32[]{:S(2)}) copy-start(bf16[3,512]{1,0:T(4,128)(2,1)} %query_ref.1) | copy-start | bytes 9220
  21.0 10.2 %collective-permute-start = (bf16[32,8,128]{2,1,0:T(8,128)(2,1)S(1)}, bf16[32,8,128]{2,1,0:T(8,128)(2,1)S(1)}, u32[]{:S(2)}, u32[]{:S(2)}) collective-permute-start(bf16[32,8,128]{2,1,0:T(8,128)(2,1)S(1)} %slice.4), channel_id=1, source_target_pairs={{1,0},{258,1},{3,2},{260,3},{5,4},{262,5},{7,6},{264,7},{9,8},{266... | collective-permute-start | bytes 196616 | tf_op jit(solution)/shard_map/ppermute | solution.py:392
  28.0 3.2 %copy-start.4 = (bf16[512,512]{1,0:T(8,128)(2,1)S(1)}, bf16[512,512]{1,0:T(8,128)(2,1)}, u32[]{:S(2)}) copy-start(bf16[512,512]{1,0:T(8,128)(2,1)} %proj_w_ref.1) | copy-start | bytes 1572868

commit v7 on v6

--- a/solution.py
+++ b/solution.py
@@ -21,13 +21,13 @@
 
 
 def member_order(members, depth=8):
-    far = [g for g in reversed(range(members)) if g % depth >= depth // 2]
-    near = sorted(
-        (g for g in range(members) if g % depth < depth // 2), key=lambda g: (g % depth, g), reverse=True
-    )
-    first = far.index(members // 2 + depth - 2)
-    far[0], far[first] = far[first], far[0]
-    return [g for pair in zip(far, near) for g in pair]
+    order = []
+    for y in range(members // depth):
+        for z in reversed(range(depth // 2)):
+            order += [y * depth + depth // 2 + z, y * depth + z]
+    first = order.index(2 * depth - 2)
+    order[0], order[first] = order[first], order[0]
+    return order
 
 
 def mul(a, b):

time: 34.3 us -> 33.2 us (0.968)
  the two profiles are of different devices: /device:TPU:8 before, /device:TPU:1 now
where the time goes in v7:
time: 33.2 us; the launch traced here: 32.8 us
  blocking collectives  20.9 us (63%)
  Pallas kernels  6.39 us (19%)
  starting transfers between devices  3.72 us (11%)
  local copies, waits for them, and re-layouts  0.92 us (3%)
  waiting for transfers between devices  0.76 us (2%)
    all_to_all x1, blocking collectives, body(): lax.all_to_all(packed.reshape(bands, 2 * SLOT, LANES), 'var', split_axis=...  20.9 us
    ppermute x1, starting transfers between devices, body(): lax.ppermute(block[:, :SLOT], ('var', 'lon'), western_pairs(bands, sectors))  3.72 us
    pallas_call x1, Pallas kernels, own_half(): pl.pallas_call(own_kernel, out_shape=[jax.ShapeDtypeStruct((HALF_ROWS, wi...  3.21 us
    pallas_call x1, Pallas kernels, window(): pl.pallas_call(window_kernel, out_shape=jax.ShapeDtypeStruct((LATENT, WLA...  2.83 us
    unnamed x18, local copies, waits for them, and re-layouts  0.92 us
    ppermute x1, waiting for transfers between devices, body(): lax.ppermute(block[:, :SLOT], ('var', 'lon'), western_pairs(bands, sectors))  0.76 us
  transfers between devices with their start and end apart: 1, of which 1 were waited for; matrix products, arithmetic and copies ran while one was open for 0% of the time, Pallas kernels for 10%

profile of v7, /device:TPU:1, one launch (start us, length us, event | category | flops | bytes accessed | tf_op | source)
XLA Modules:
  0.0 32.8 jit_solution(15415371203485592549)
XLA Ops:
  0.0 0.0 copy-start.5
  0.0 0.9 %copy-done.5 = bf16[1,768,48]{1,2,0:T(8,128)(2,1)S(1)} copy-done((bf16[1,768,48]{1,2,0:T(8,128)(2,1)S(1)}, bf16[1,768,48]{1,2,0:T(8,128)(2,1)}, u32[]{:S(2)}) %copy-start.5) | copy-done | bytes 73752
  0.9 0.0 copy-start
  0.9 0.0 copy-start.1
  0.9 0.0 copy-start.2
  0.9 0.0 copy-start.3
  0.9 0.0 copy-start.6
  0.9 0.0 copy-start.7
  0.9 0.0 copy-start.8
  0.9 0.3 %pack.1 = bf16[512,128]{1,0:T(8,128)(2,1)S(1)} custom-call(bf16[48,768]{1,0:T(8,128)(2,1)S(1)} %bitcast.9), custom_call_target="tpu_custom_call" | custom-call | flops 8000000000 | bytes 200000 | tf_op jit(solution)/shard_map/pack/pallas_call | solution.py:311
  1.3 20.9 %all_to_all.5 = bf16[32,16,128]{2,1,0:T(8,128)(2,1)S(1)} all-to-all(bf16[32,16,128]{2,1,0:T(8,128)(2,1)S(1)} %bitcast.8), channel_id=1, replica_groups={{224,48,96,32,80,16,64,0,240,176,112,160,208,144,192,128,368,304,352,28..., dimensions={0} | all-to-all | bytes 262144 | tf_op jit(solution)/shard_map/all_to_all | solution.py:384
  22.2 3.7 %collective-permute-start = (bf16[32,8,128]{2,1,0:T(8,128)(2,1)S(1)}, bf16[32,8,128]{2,1,0:T(8,128)(2,1)S(1)}, u32[]{:S(2)}, u32[]{:S(2)}) collective-permute-start(bf16[32,8,128]{2,1,0:T(8,128)(2,1)S(1)} %slice.4), channel_id=1, source_target_pairs={{1,0},{258,1},{3,2},{260,3},{5,4},{262,5},{7,6},{264,7},{9,8},{266... | collective-permute-start | bytes 196616 | tf_op jit(solution)/shard_map/ppermute | solution.py:392
  25.9 0.0 copy-done
  25.9 0.0 copy-done.1
  25.9 0.0 copy-done.2
  25.9 0.0 copy-done.3
  25.9 0.0 copy-done.6
  26.0 0.0 copy-done.7
  26.0 0.0 copy-done.8
  26.0 0.0 copy-start.4
  26.0 3.2 %own_half.1 = (f32[112,512]{1,0:T(8,128)S(1)}, bf16[112,1536]{1,0:T(8,128)(2,1)S(1)}, bf16[256,768]{1,0:T(8,128)(2,1)S(1)}, bf16[512,768]{1,0:T(8,128)(2,1)S(1)}...) custom-call(bf16[512,128]{1,0:T(8,128)(2,1)S(1)} %bitcast.7, ...), custom_call_target="tpu_custom_call" | custom-call | flops 4000000000 | bytes 2000000 | tf_op jit(solution)/shard_map/own_half/pallas_call | solution.py:333
  29.2 0.8 %collective-permute-done = bf16[32,8,128]{2,1,0:T(8,128)(2,1)S(1)} collective-permute-done((bf16[32,8,128]{2,1,0:T(8,128)(2,1)S(1)}, bf16[32,8,128]{2,1,0:T(8,128)(2,1)S(1)}, u32[]{:S(2)}, u32[]{:S(2)}) %collective-permute-start) | collective-permute-done | bytes 65568 | tf_op jit(solution)/shard_map/ppermute | solution.py:392
  30.0 0.0 copy-done.4
  30.0 2.8 %window.1 = bf16[3,6,12,512]{3,2,1,0:T(8,128)(2,1)} custom-call(bf16[256,128]{1,0:T(8,128)(2,1)S(1)} %bitcast.11, f32[112,512]{1,0:T(8,128)S(1)} %get-tuple-element.14.shifted_ref, bf16[112,1536]{1,0:T(8,128)(2,1)S(1)} %get-tuple-element.15.qkv_ref, bf16[256,768]{1,0:T(8,128)(2,1)S(1)} %get-tuple-element.16.folded_ref, ...), custom_call_target="tpu_custom_call" | custom-call | flops 8000000000 | bytes 4000000 | tf_op jit(solution)/shard_map/window/pallas_call | solution.py:360
  (1 shorter events, 0.0 us)
Async XLA Ops:
  0.0 0.9 %copy-start.5 = (bf16[1,768,48]{1,2,0:T(8,128)(2,1)S(1)}, bf16[1,768,48]{1,2,0:T(8,128)(2,1)}, u32[]{:S(2)}) copy-start(bf16[1,768,48]{1,2,0:T(8,128)(2,1)} %param.9) | copy-start | bytes 221188
  0.9 25.0 %copy-start = (bf16[512,1536]{1,0:T(8,128)(2,1)S(1)}, bf16[512,1536]{1,0:T(8,128)(2,1)}, u32[]{:S(2)}) copy-start(bf16[512,1536]{1,0:T(8,128)(2,1)} %qkv_w_ref.1) | copy-start | bytes 4718596
  0.9 25.0 %copy-start.1 = (bf16[512,512]{1,0:T(8,128)(2,1)S(1)}, bf16[512,512]{1,0:T(8,128)(2,1)}, u32[]{:S(2)}) copy-start(bf16[512,512]{1,0:T(8,128)(2,1)} %key_ref.1) | copy-start | bytes 1572868
  0.9 25.0 %copy-start.2 = (bf16[512,512]{1,0:T(8,128)(2,1)S(1)}, bf16[512,512]{1,0:T(8,128)(2,1)}, u32[]{:S(2)}) copy-start(bf16[512,512]{1,0:T(8,128)(2,1)} %value_ref.1) | copy-start | bytes 1572868
  0.9 25.0 %copy-start.3 = (bf16[512,512]{1,0:T(8,128)(2,1)S(1)}, bf16[512,512]{1,0:T(8,128)(2,1)}, u32[]{:S(2)}) copy-start(bf16[512,512]{1,0:T(8,128)(2,1)} %out_w_ref.3) | copy-start | bytes 1572868
  0.9 25.1 %copy-start.6 = (bf16[4,16,512]{2,1,0:T(8,128)(2,1)S(1)}, bf16[4,16,512]{2,1,0:T(8,128)(2,1)}, u32[]{:S(2)}) copy-start(bf16[4,16,512]{2,1,0:T(8,128)(2,1)} %param.10) | copy-start | bytes 196612
  0.9 25.1 %copy-start.7 = (f32[8,512]{1,0:T(8,128)S(1)}, f32[8,512]{1,0:T(8,128)}, u32[]{:S(2)}) copy-start(f32[8,512]{1,0:T(8,128)} %level_ref.1) | copy-start | bytes 49156
  0.9 25.1 %copy-start.8 = (bf16[3,512]{1,0:T(4,128)(2,1)S(1)}, bf16[3,512]{1,0:T(4,128)(2,1)}, u32[]{:S(2)}) copy-start(bf16[3,512]{1,0:T(4,128)(2,1)} %query_ref.1) | copy-start | bytes 9220
  22.2 7.8 %collective-permute-start = (bf16[32,8,128]{2,1,0:T(8,128)(2,1)S(1)}, bf16[32,8,128]{2,1,0:T(8,128)(2,1)S(1)}, u32[]{:S(2)}, u32[]{:S(2)}) collective-permute-start(bf16[32,8,128]{2,1,0:T(8,128)(2,1)S(1)} %slice.4), channel_id=1, source_target_pairs={{1,0},{258,1},{3,2},{260,3},{5,4},{262,5},{7,6},{264,7},{9,8},{266... | collective-permute-start | bytes 196616 | tf_op jit(solution)/shard_map/ppermute | solution.py:392
  26.0 4.0 %copy-start.4 = (bf16[512,512]{1,0:T(8,128)(2,1)S(1)}, bf16[512,512]{1,0:T(8,128)(2,1)}, u32[]{:S(2)}) copy-start(bf16[512,512]{1,0:T(8,128)(2,1)} %proj_w_ref.1) | copy-start | bytes 1572868

commit v8 on v7

--- a/solution.py
+++ b/solution.py
@@ -220,7 +220,7 @@
 def tokens_of(attended, slots, clean, out_weight, through, base, queries):
     width = attended.shape[1]
     for c in range(width // LANES):
-        slots[c] = attended[:, c * LANES : (c + 1) * LANES]
+        slots[c, pl.ds(0, attended.shape[0]), :] = attended[:, c * LANES : (c + 1) * LANES]
     pairs = LATENT * WLAT
     for q in range(LATENT):
         for a in range(WLAT):
@@ -322,7 +322,7 @@
 
 def scratch(width):
     return [
-        pltpu.VMEM((width // LANES, LATENT * HALF * SLOT, LANES), F32),
+        pltpu.VMEM((width // LANES, LATENT * HALF * SLOT + 3 * SLOT, LANES), F32),
         pltpu.VMEM((HALF_ROWS, width), F32),
     ]
 

time: 33.2 us -> 33.2 us (level)
  no operation moved by 1% of the time
where the time goes in v8:
time: 33.2 us; the launch traced here: 32.8 us
  blocking collectives  20.9 us (63%)
  Pallas kernels  6.39 us (19%)
  starting transfers between devices  3.72 us (11%)
  local copies, waits for them, and re-layouts  0.92 us (3%)
  waiting for transfers between devices  0.76 us (2%)
    all_to_all x1, blocking collectives, body(): lax.all_to_all(packed.reshape(bands, 2 * SLOT, LANES), 'var', split_axis=...  20.9 us
    ppermute x1, starting transfers between devices, body(): lax.ppermute(block[:, :SLOT], ('var', 'lon'), western_pairs(bands, sectors))  3.72 us
    pallas_call x1, Pallas kernels, own_half(): pl.pallas_call(own_kernel, out_shape=[jax.ShapeDtypeStruct((HALF_ROWS, wi...  3.21 us
    pallas_call x1, Pallas kernels, window(): pl.pallas_call(window_kernel, out_shape=jax.ShapeDtypeStruct((LATENT, WLA...  2.83 us
    unnamed x18, local copies, waits for them, and re-layouts  0.92 us
    ppermute x1, waiting for transfers between devices, body(): lax.ppermute(block[:, :SLOT], ('var', 'lon'), western_pairs(bands, sectors))  0.76 us
  transfers between devices with their start and end apart: 1, of which 1 were waited for; matrix products, arithmetic and copies ran while one was open for 0% of the time, Pallas kernels for 10%

profile of v8, /device:TPU:1, one launch (start us, length us, event | category | flops | bytes accessed | tf_op | source)
XLA Modules:
  0.0 32.8 jit_solution(400953450227603398)
XLA Ops:
  0.0 0.0 copy-start.5
  0.0 0.9 %copy-done.5 = bf16[1,768,48]{1,2,0:T(8,128)(2,1)S(1)} copy-done((bf16[1,768,48]{1,2,0:T(8,128)(2,1)S(1)}, bf16[1,768,48]{1,2,0:T(8,128)(2,1)}, u32[]{:S(2)}) %copy-start.5) | copy-done | bytes 73752
  0.9 0.0 copy-start
  0.9 0.0 copy-start.1
  0.9 0.0 copy-start.2
  0.9 0.0 copy-start.3
  0.9 0.0 copy-start.6
  0.9 0.0 copy-start.7
  0.9 0.0 copy-start.8
  0.9 0.3 %pack.1 = bf16[512,128]{1,0:T(8,128)(2,1)S(1)} custom-call(bf16[48,768]{1,0:T(8,128)(2,1)S(1)} %bitcast.9), custom_call_target="tpu_custom_call" | custom-call | flops 8000000000 | bytes 200000 | tf_op jit(solution)/shard_map/pack/pallas_call | solution.py:311
  1.3 20.9 %all_to_all.5 = bf16[32,16,128]{2,1,0:T(8,128)(2,1)S(1)} all-to-all(bf16[32,16,128]{2,1,0:T(8,128)(2,1)S(1)} %bitcast.8), channel_id=1, replica_groups={{224,48,96,32,80,16,64,0,240,176,112,160,208,144,192,128,368,304,352,28..., dimensions={0} | all-to-all | bytes 262144 | tf_op jit(solution)/shard_map/all_to_all | solution.py:384
  22.2 3.7 %collective-permute-start = (bf16[32,8,128]{2,1,0:T(8,128)(2,1)S(1)}, bf16[32,8,128]{2,1,0:T(8,128)(2,1)S(1)}, u32[]{:S(2)}, u32[]{:S(2)}) collective-permute-start(bf16[32,8,128]{2,1,0:T(8,128)(2,1)S(1)} %slice.4), channel_id=1, source_target_pairs={{1,0},{258,1},{3,2},{260,3},{5,4},{262,5},{7,6},{264,7},{9,8},{266... | collective-permute-start | bytes 196616 | tf_op jit(solution)/shard_map/ppermute | solution.py:392
  25.9 0.0 copy-done
  25.9 0.0 copy-done.1
  25.9 0.0 copy-done.2
  25.9 0.0 copy-done.3
  25.9 0.0 copy-done.6
  26.0 0.0 copy-done.7
  26.0 0.0 copy-done.8
  26.0 0.0 copy-start.4
  26.0 3.2 %own_half.1 = (f32[112,512]{1,0:T(8,128)S(1)}, bf16[112,1536]{1,0:T(8,128)(2,1)S(1)}, bf16[256,768]{1,0:T(8,128)(2,1)S(1)}, bf16[512,768]{1,0:T(8,128)(2,1)S(1)}...) custom-call(bf16[512,128]{1,0:T(8,128)(2,1)S(1)} %bitcast.7, ...), custom_call_target="tpu_custom_call" | custom-call | flops 4000000000 | bytes 2000000 | tf_op jit(solution)/shard_map/own_half/pallas_call | solution.py:333
  29.2 0.8 %collective-permute-done = bf16[32,8,128]{2,1,0:T(8,128)(2,1)S(1)} collective-permute-done((bf16[32,8,128]{2,1,0:T(8,128)(2,1)S(1)}, bf16[32,8,128]{2,1,0:T(8,128)(2,1)S(1)}, u32[]{:S(2)}, u32[]{:S(2)}) %collective-permute-start) | collective-permute-done | bytes 65568 | tf_op jit(solution)/shard_map/ppermute | solution.py:392
  30.0 0.0 copy-done.4
  30.0 2.8 %window.1 = bf16[3,6,12,512]{3,2,1,0:T(8,128)(2,1)} custom-call(bf16[256,128]{1,0:T(8,128)(2,1)S(1)} %bitcast.11, f32[112,512]{1,0:T(8,128)S(1)} %get-tuple-element.14.shifted_ref, bf16[112,1536]{1,0:T(8,128)(2,1)S(1)} %get-tuple-element.15.qkv_ref, bf16[256,768]{1,0:T(8,128)(2,1)S(1)} %get-tuple-element.16.folded_ref, ...), custom_call_target="tpu_custom_call" | custom-call | flops 8000000000 | bytes 4000000 | tf_op jit(solution)/shard_map/window/pallas_call | solution.py:360
  (1 shorter events, 0.0 us)
Async XLA Ops:
  0.0 0.9 %copy-start.5 = (bf16[1,768,48]{1,2,0:T(8,128)(2,1)S(1)}, bf16[1,768,48]{1,2,0:T(8,128)(2,1)}, u32[]{:S(2)}) copy-start(bf16[1,768,48]{1,2,0:T(8,128)(2,1)} %param.9) | copy-start | bytes 221188
  0.9 25.0 %copy-start = (bf16[512,1536]{1,0:T(8,128)(2,1)S(1)}, bf16[512,1536]{1,0:T(8,128)(2,1)}, u32[]{:S(2)}) copy-start(bf16[512,1536]{1,0:T(8,128)(2,1)} %qkv_w_ref.1) | copy-start | bytes 4718596
  0.9 25.0 %copy-start.1 = (bf16[512,512]{1,0:T(8,128)(2,1)S(1)}, bf16[512,512]{1,0:T(8,128)(2,1)}, u32[]{:S(2)}) copy-start(bf16[512,512]{1,0:T(8,128)(2,1)} %key_ref.1) | copy-start | bytes 1572868
  0.9 25.0 %copy-start.2 = (bf16[512,512]{1,0:T(8,128)(2,1)S(1)}, bf16[512,512]{1,0:T(8,128)(2,1)}, u32[]{:S(2)}) copy-start(bf16[512,512]{1,0:T(8,128)(2,1)} %value_ref.1) | copy-start | bytes 1572868
  0.9 25.0 %copy-start.3 = (bf16[512,512]{1,0:T(8,128)(2,1)S(1)}, bf16[512,512]{1,0:T(8,128)(2,1)}, u32[]{:S(2)}) copy-start(bf16[512,512]{1,0:T(8,128)(2,1)} %out_w_ref.3) | copy-start | bytes 1572868
  0.9 25.1 %copy-start.6 = (bf16[4,16,512]{2,1,0:T(8,128)(2,1)S(1)}, bf16[4,16,512]{2,1,0:T(8,128)(2,1)}, u32[]{:S(2)}) copy-start(bf16[4,16,512]{2,1,0:T(8,128)(2,1)} %param.10) | copy-start | bytes 196612
  0.9 25.1 %copy-start.7 = (f32[8,512]{1,0:T(8,128)S(1)}, f32[8,512]{1,0:T(8,128)}, u32[]{:S(2)}) copy-start(f32[8,512]{1,0:T(8,128)} %level_ref.1) | copy-start | bytes 49156
  0.9 25.1 %copy-start.8 = (bf16[3,512]{1,0:T(4,128)(2,1)S(1)}, bf16[3,512]{1,0:T(4,128)(2,1)}, u32[]{:S(2)}) copy-start(bf16[3,512]{1,0:T(4,128)(2,1)} %query_ref.1) | copy-start | bytes 9220
  22.2 7.8 %collective-permute-start = (bf16[32,8,128]{2,1,0:T(8,128)(2,1)S(1)}, bf16[32,8,128]{2,1,0:T(8,128)(2,1)S(1)}, u32[]{:S(2)}, u32[]{:S(2)}) collective-permute-start(bf16[32,8,128]{2,1,0:T(8,128)(2,1)S(1)} %slice.4), channel_id=1, source_target_pairs={{1,0},{258,1},{3,2},{260,3},{5,4},{262,5},{7,6},{264,7},{9,8},{266... | collective-permute-start | bytes 196616 | tf_op jit(solution)/shard_map/ppermute | solution.py:392
  26.0 4.0 %copy-start.4 = (bf16[512,512]{1,0:T(8,128)(2,1)S(1)}, bf16[512,512]{1,0:T(8,128)(2,1)}, u32[]{:S(2)}) copy-start(bf16[512,512]{1,0:T(8,128)(2,1)} %proj_w_ref.1) | copy-start | bytes 1572868

commit v9 on v8

--- a/solution.py
+++ b/solution.py
@@ -264,7 +264,7 @@
 
 def window_kernel(
     block_ref, shifted_ref, qkv_ref, folded_ref, gather_ref, marks_ref, spread_ref, through_ref,
-    base_ref, rows_ref, out_w_ref, proj_w_ref, out_ref, slots, clean, result,
+    base_ref, rows_ref, out_w_ref, proj_w_ref, out_hbm, slots, clean, result, out_ref, sent,
 ):
     fields = block_ref.shape[0] // SLOT
     width = out_w_ref.shape[0]
@@ -295,10 +295,15 @@
         both = jnp.where(jnp.concatenate([first, first], axis=1), found[0], found[1])
         mixed.append((both[:, :LANES] / both[:, LANES:] * 2.0**8).astype(BF16))
     result[...] = shifted + mul(jnp.concatenate(mixed, axis=1), proj_w_ref[...])
+    copies = [pltpu.make_async_copy(out_ref.at[q], out_hbm.at[q], sent.at[q]) for q in range(LATENT)]
     for i in range(pairs):
         out_ref[i // WLAT, i % WLAT] = jnp.concatenate(
             [result[pl.ds(i * HALF, HALF), :], result[pl.ds(HALF_ROWS + i * HALF, HALF), :]], axis=0
         ).astype(BF16)
+        if i % WLAT == WLAT - 1:
+            copies[i // WLAT].start()
+    for copy in copies:
+        copy.wait()
 
 
 def whole(count):
@@ -361,8 +366,13 @@
         window_kernel,
         out_shape=jax.ShapeDtypeStruct((LATENT, WLAT, WLON, width), BF16),
         in_specs=whole(12),
-        out_specs=whole(1)[0],
-        scratch_shapes=scratch(width) + [pltpu.VMEM((2 * HALF_ROWS, width), F32)],
+        out_specs=pl.BlockSpec(memory_space=pltpu.HBM),
+        scratch_shapes=scratch(width)
+        + [
+            pltpu.VMEM((2 * HALF_ROWS, width), F32),
+            pltpu.VMEM((LATENT, WLAT, WLON, width), BF16),
+            pltpu.SemaphoreType.DMA((LATENT,)),
+        ],
         compiler_params=pltpu.CompilerParams(vmem_limit_bytes=32 * 2**20),
         cost_estimate=pl.CostEstimate(flops=8 * 10**9, bytes_accessed=4 * 10**6, transcendentals=0),
         name="window",

time: 33.2 us -> 33.2 us (level)
  no operation moved by 1% of the time
where the time goes in v9:
time: 33.2 us; the launch traced here: 32.8 us
  blocking collectives  20.9 us (63%)
  Pallas kernels  6.38 us (19%)
  starting transfers between devices  3.72 us (11%)
  local copies, waits for them, and re-layouts  0.92 us (3%)
  waiting for transfers between devices  0.76 us (2%)
    all_to_all x1, blocking collectives, body(): lax.all_to_all(packed.reshape(bands, 2 * SLOT, LANES), 'var', split_axis=...  20.9 us
    ppermute x1, starting transfers between devices, body(): lax.ppermute(block[:, :SLOT], ('var', 'lon'), western_pairs(bands, sectors))  3.72 us
    pallas_call x1, Pallas kernels, own_half(): pl.pallas_call(own_kernel, out_shape=[jax.ShapeDtypeStruct((HALF_ROWS, wi...  3.21 us
    pallas_call x1, Pallas kernels, window(): pl.pallas_call(window_kernel, out_shape=jax.ShapeDtypeStruct((LATENT, WLA...  2.82 us
    unnamed x18, local copies, waits for them, and re-layouts  0.92 us
    ppermute x1, waiting for transfers between devices, body(): lax.ppermute(block[:, :SLOT], ('var', 'lon'), western_pairs(bands, sectors))  0.76 us
  transfers between devices with their start and end apart: 1, of which 1 were waited for; matrix products, arithmetic and copies ran while one was open for 0% of the time, Pallas kernels for 10%

profile of v9, /device:TPU:1, one launch (start us, length us, event | category | flops | bytes accessed | tf_op | source)
XLA Modules:
  0.0 32.8 jit_solution(5830801011582103041)
XLA Ops:
  0.0 0.0 copy-start.5
  0.0 0.9 %copy-done.5 = bf16[1,768,48]{1,2,0:T(8,128)(2,1)S(1)} copy-done((bf16[1,768,48]{1,2,0:T(8,128)(2,1)S(1)}, bf16[1,768,48]{1,2,0:T(8,128)(2,1)}, u32[]{:S(2)}) %copy-start.5) | copy-done | bytes 73752
  0.9 0.0 copy-start
  0.9 0.0 copy-start.1
  0.9 0.0 copy-start.2
  0.9 0.0 copy-start.3
  0.9 0.0 copy-start.6
  0.9 0.0 copy-start.7
  0.9 0.0 copy-start.8
  0.9 0.3 %pack.1 = bf16[512,128]{1,0:T(8,128)(2,1)S(1)} custom-call(bf16[48,768]{1,0:T(8,128)(2,1)S(1)} %bitcast.9), custom_call_target="tpu_custom_call" | custom-call | flops 8000000000 | bytes 200000 | tf_op jit(solution)/shard_map/pack/pallas_call | solution.py:316
  1.3 20.9 %all_to_all.5 = bf16[32,16,128]{2,1,0:T(8,128)(2,1)S(1)} all-to-all(bf16[32,16,128]{2,1,0:T(8,128)(2,1)S(1)} %bitcast.8), channel_id=1, replica_groups={{224,48,96,32,80,16,64,0,240,176,112,160,208,144,192,128,368,304,352,28..., dimensions={0} | all-to-all | bytes 262144 | tf_op jit(solution)/shard_map/all_to_all | solution.py:394
  22.2 3.7 %collective-permute-start = (bf16[32,8,128]{2,1,0:T(8,128)(2,1)S(1)}, bf16[32,8,128]{2,1,0:T(8,128)(2,1)S(1)}, u32[]{:S(2)}, u32[]{:S(2)}) collective-permute-start(bf16[32,8,128]{2,1,0:T(8,128)(2,1)S(1)} %slice.4), channel_id=1, source_target_pairs={{1,0},{258,1},{3,2},{260,3},{5,4},{262,5},{7,6},{264,7},{9,8},{266... | collective-permute-start | bytes 196616 | tf_op jit(solution)/shard_map/ppermute | solution.py:402
  25.9 0.0 copy-done
  25.9 0.0 copy-done.1
  25.9 0.0 copy-done.2
  25.9 0.0 copy-done.3
  25.9 0.0 copy-done.6
  26.0 0.0 copy-done.7
  26.0 0.0 copy-done.8
  26.0 0.0 copy-start.4
  26.0 3.2 %own_half.1 = (f32[112,512]{1,0:T(8,128)S(1)}, bf16[112,1536]{1,0:T(8,128)(2,1)S(1)}, bf16[256,768]{1,0:T(8,128)(2,1)S(1)}, bf16[512,768]{1,0:T(8,128)(2,1)S(1)}...) custom-call(bf16[512,128]{1,0:T(8,128)(2,1)S(1)} %bitcast.7, ...), custom_call_target="tpu_custom_call" | custom-call | flops 4000000000 | bytes 2000000 | tf_op jit(solution)/shard_map/own_half/pallas_call | solution.py:338
  29.2 0.8 %collective-permute-done = bf16[32,8,128]{2,1,0:T(8,128)(2,1)S(1)} collective-permute-done((bf16[32,8,128]{2,1,0:T(8,128)(2,1)S(1)}, bf16[32,8,128]{2,1,0:T(8,128)(2,1)S(1)}, u32[]{:S(2)}, u32[]{:S(2)}) %collective-permute-start) | collective-permute-done | bytes 65568 | tf_op jit(solution)/shard_map/ppermute | solution.py:402
  30.0 0.0 copy-done.4
  30.0 2.8 %window.1 = bf16[3,6,12,512]{3,2,1,0:T(8,128)(2,1)} custom-call(bf16[256,128]{1,0:T(8,128)(2,1)S(1)} %bitcast.11, f32[112,512]{1,0:T(8,128)S(1)} %get-tuple-element.14.shifted_ref, bf16[112,1536]{1,0:T(8,128)(2,1)S(1)} %get-tuple-element.15.qkv_ref, bf16[256,768]{1,0:T(8,128)(2,1)S(1)} %get-tuple-element.16.folded_ref, ...), custom_call_target="tpu_custom_call" | custom-call | flops 8000000000 | bytes 4000000 | tf_op jit(solution)/shard_map/window/pallas_call | solution.py:365
  (1 shorter events, 0.0 us)
Async XLA Ops:
  0.0 0.9 %copy-start.5 = (bf16[1,768,48]{1,2,0:T(8,128)(2,1)S(1)}, bf16[1,768,48]{1,2,0:T(8,128)(2,1)}, u32[]{:S(2)}) copy-start(bf16[1,768,48]{1,2,0:T(8,128)(2,1)} %param.9) | copy-start | bytes 221188
  0.9 25.0 %copy-start = (bf16[512,1536]{1,0:T(8,128)(2,1)S(1)}, bf16[512,1536]{1,0:T(8,128)(2,1)}, u32[]{:S(2)}) copy-start(bf16[512,1536]{1,0:T(8,128)(2,1)} %qkv_w_ref.1) | copy-start | bytes 4718596
  0.9 25.0 %copy-start.1 = (bf16[512,512]{1,0:T(8,128)(2,1)S(1)}, bf16[512,512]{1,0:T(8,128)(2,1)}, u32[]{:S(2)}) copy-start(bf16[512,512]{1,0:T(8,128)(2,1)} %key_ref.1) | copy-start | bytes 1572868
  0.9 25.0 %copy-start.2 = (bf16[512,512]{1,0:T(8,128)(2,1)S(1)}, bf16[512,512]{1,0:T(8,128)(2,1)}, u32[]{:S(2)}) copy-start(bf16[512,512]{1,0:T(8,128)(2,1)} %value_ref.1) | copy-start | bytes 1572868
  0.9 25.0 %copy-start.3 = (bf16[512,512]{1,0:T(8,128)(2,1)S(1)}, bf16[512,512]{1,0:T(8,128)(2,1)}, u32[]{:S(2)}) copy-start(bf16[512,512]{1,0:T(8,128)(2,1)} %out_w_ref.3) | copy-start | bytes 1572868
  0.9 25.1 %copy-start.6 = (bf16[4,16,512]{2,1,0:T(8,128)(2,1)S(1)}, bf16[4,16,512]{2,1,0:T(8,128)(2,1)}, u32[]{:S(2)}) copy-start(bf16[4,16,512]{2,1,0:T(8,128)(2,1)} %param.10) | copy-start | bytes 196612
  0.9 25.1 %copy-start.7 = (f32[8,512]{1,0:T(8,128)S(1)}, f32[8,512]{1,0:T(8,128)}, u32[]{:S(2)}) copy-start(f32[8,512]{1,0:T(8,128)} %level_ref.1) | copy-start | bytes 49156
  0.9 25.1 %copy-start.8 = (bf16[3,512]{1,0:T(4,128)(2,1)S(1)}, bf16[3,512]{1,0:T(4,128)(2,1)}, u32[]{:S(2)}) copy-start(bf16[3,512]{1,0:T(4,128)(2,1)} %query_ref.1) | copy-start | bytes 9220
  22.2 7.8 %collective-permute-start = (bf16[32,8,128]{2,1,0:T(8,128)(2,1)S(1)}, bf16[32,8,128]{2,1,0:T(8,128)(2,1)S(1)}, u32[]{:S(2)}, u32[]{:S(2)}) collective-permute-start(bf16[32,8,128]{2,1,0:T(8,128)(2,1)S(1)} %slice.4), channel_id=1, source_target_pairs={{1,0},{258,1},{3,2},{260,3},{5,4},{262,5},{7,6},{264,7},{9,8},{266... | collective-permute-start | bytes 196616 | tf_op jit(solution)/shard_map/ppermute | solution.py:402
  26.0 4.0 %copy-start.4 = (bf16[512,512]{1,0:T(8,128)(2,1)S(1)}, bf16[512,512]{1,0:T(8,128)(2,1)}, u32[]{:S(2)}) copy-start(bf16[512,512]{1,0:T(8,128)(2,1)} %proj_w_ref.1) | copy-start | bytes 1572868
